TPU v7x, 32 devices: a whole 2x2x4 slice. The times are simulated.
32 devices in a mesh: width: 4 (over y, core), dp: 8 (over z, x).
Axes of the slice: x: 2, y: 2, z: 4, core: 2. Of those that a mesh axis runs over, the one named last changes fastest.
Arguments:
- inputs: bfloat16 [4, 8192, 768], P('width', 'dp'), may hold values from -6 to 6
- cotangent: bfloat16 [4, 8192, 768], P('width', 'dp'), may hold values from -6 to 6
- replacement_ids: int32 [4, 8192], P('width', 'dp'), may hold values from 0 to 1023
- augmented_count: int32 [4, 8], P('width', 'dp'), may hold values from 0 to 1024
- segment_ids: int32 [4, 8, 1024], P('width', 'dp'), may hold values from 0 to 3, never falling along the last dimension, each value on 1 to 512 neighbouring positions
- query_weight: bfloat16 [768, 768], P('dp'), may hold values from -0.21875 to 0.21875
- key_weight: bfloat16 [768, 768], P('dp'), may hold values from -0.21875 to 0.21875
- value_weight: bfloat16 [768, 768], P('dp'), may hold values from -0.21875 to 0.21875
- output_weight: bfloat16 [768, 768], P('dp'), may hold values from -2.5 to 2.5
- inner_weight: bfloat16 [768, 3072], P('dp'), may hold values from -0.21875 to 0.21875
- outer_weight: bfloat16 [3072, 768], P('dp'), may hold values from -0.15625 to 0.15625
- query_bias: bfloat16 [768], P('dp'), may hold values from -3 to 3
- value_bias: bfloat16 [768], P('dp'), may hold values from -3 to 3
- output_bias: bfloat16 [768], P('dp'), may hold values from -3 to 3
- inner_bias: bfloat16 [3072], P('dp'), may hold values from -3 to 3
- outer_bias: bfloat16 [768], P('dp'), may hold values from -3 to 3
- attention_gain: bfloat16 [768], P('dp'), may hold values from 0.25 to 1.75
- attention_shift: bfloat16 [768], P('dp'), may hold values from -3 to 3
- feed_gain: bfloat16 [768], P('dp'), may hold values from 0.25 to 1.75
- feed_shift: bfloat16 [768], P('dp'), may hold values from -3 to 3
Outputs:
- block_output: bfloat16 [4, 8192, 768], P('width', 'dp')
- input_gradient: float32 [4, 8192, 768], P('width', 'dp')
- grad_query_weight: float32 [768, 768], P('dp')
- grad_key_weight: float32 [768, 768], P('dp')
- grad_value_weight: float32 [768, 768], P('dp')
- grad_output_weight: float32 [768, 768], P('dp')
- grad_inner_weight: float32 [768, 3072], P('dp')
- grad_outer_weight: float32 [3072, 768], P('dp')
- grad_query_bias: float32 [768], P('dp')
- grad_value_bias: float32 [768], P('dp')
- grad_output_bias: float32 [768], P('dp')
- grad_inner_bias: float32 [3072], P('dp')
- grad_outer_bias: float32 [768], P('dp')
- grad_attention_gain: float32 [768], P('dp')
- grad_attention_shift: float32 [768], P('dp')
- grad_feed_gain: float32 [768], P('dp')
- grad_feed_shift: float32 [768], P('dp')
Inputs may be any that keep to these rules, and one draw needn't show every extreme that they name: `replacement_ids`: a position within the token's own sequence. `segment_ids`: never falling along a sequence; each document spans 1 to 512 positions.
All inputs are finite; a program needn't handle non-finite values.
Results may differ from a plain program's by a relative error of at most 0.013.
The roundings to bfloat16 on the way count: a program that leaves them out, or rounds other values in their place, can miss the bound.
Values may be sent and summed in bfloat16 or wider, within the bound.
No kernel may reach another device: no remote copies, remote signals or barrier semaphores. Data moves between devices by JAX's collectives and lax.ppermute only.
A program may use at most 256 MiB of HBM per device.

v0:
```python
import jax
import jax.numpy as jnp
from jax import lax
from jax.sharding import PartitionSpec as P

HEADS = 12
HEAD_DIM = 64
FF = 3072


EPSILON = 1e-12
NEGATIVE = -1000000000.0


def layer_norm(hidden, scaling, offset):
    average = jnp.mean(hidden, axis=-1, keepdims=True)
    centred = hidden - average
    variance = jnp.mean(centred * centred, axis=-1, keepdims=True)
    return centred * lax.rsqrt(variance + EPSILON) * scaling + offset


def gelu_exact(values):
    return jax.nn.gelu(values, approximate=False)


def product(matrix, second):
    return jnp.dot(matrix, second, preferred_element_type=jnp.float32)


def transposed_times(matrix, second):
    return lax.dot_general(
        matrix, second, (((0,), (0,)), ((), ())), preferred_element_type=jnp.float32
    )


def times_transposed(matrix, second):
    return lax.dot_general(
        matrix, second, (((1,), (1,)), ((), ())), preferred_element_type=jnp.float32
    )


def column_sums(matrix):
    return jnp.sum(matrix.astype(jnp.float32), axis=0)


def per_device(
    inputs,
    cotangent,
    replacement_ids,
    augmented_count,
    segment_ids,
    query_weight,
    key_weight,
    value_weight,
    output_weight,
    inner_weight,
    outer_weight,
    query_bias,
    value_bias,
    output_bias,
    inner_bias,
    outer_bias,
    attention_gain,
    attention_shift,
    feed_gain,
    feed_shift,
):
    gathered = (
        lax.all_gather(query_weight, "dp", axis=0, tiled=True),
        lax.all_gather(key_weight, "dp", axis=0, tiled=True),
        lax.all_gather(value_weight, "dp", axis=0, tiled=True),
        lax.all_gather(output_weight, "dp", axis=0, tiled=True),
        lax.all_gather(inner_weight, "dp", axis=0, tiled=True),
        lax.all_gather(outer_weight, "dp", axis=0, tiled=True),
        lax.all_gather(query_bias, "dp", axis=0, tiled=True),
        lax.all_gather(value_bias, "dp", axis=0, tiled=True),
        lax.all_gather(output_bias, "dp", axis=0, tiled=True),
        lax.all_gather(inner_bias, "dp", axis=0, tiled=True),
        lax.all_gather(outer_bias, "dp", axis=0, tiled=True),
        lax.all_gather(attention_gain, "dp", axis=0, tiled=True),
        lax.all_gather(attention_shift, "dp", axis=0, tiled=True),
        lax.all_gather(feed_gain, "dp", axis=0, tiled=True),
        lax.all_gather(feed_shift, "dp", axis=0, tiled=True),
    )
    (
        query_full,
        key_full,
        value_full,
        output_full,
        inner_full,
        outer_full,
        query_bias_full,
        value_bias_full,
        output_bias_full,
        inner_bias_full,
        outer_bias_full,
        gain_first,
        shift_first,
        gain_second,
        shift_second,
    ) = gathered
    row_total = inputs.shape[1]
    width_model = inputs.shape[2]
    width_index = lax.axis_index("width")
    group_total = lax.axis_size("width")
    head_keep = (jnp.arange(HEADS) < HEADS * (width_index + 1) // group_total).astype(jnp.float32)
    unit_keep = (jnp.arange(FF) < FF * (width_index + 1) // group_total).astype(jnp.float32)
    score_scale = HEAD_DIM ** (-0.5)
    block_rows = min(512, row_total)
    block_total = row_total // block_rows
    positions = jnp.arange(row_total, dtype=jnp.int32)
    sources = jnp.where(positions < augmented_count[0, 0], replacement_ids[0], positions)
    mixed_low = jnp.take(inputs[0], sources, axis=0)
    mixed_rows = mixed_low.astype(jnp.float32)
    queries = (product(mixed_low, query_full) + query_bias_full).astype(jnp.bfloat16)
    key_heads = (
        product(mixed_low, key_full).astype(jnp.bfloat16).reshape(row_total, HEADS, HEAD_DIM)
    )
    value_heads = (
        (product(mixed_low, value_full) + value_bias_full)
        .astype(jnp.bfloat16)
        .reshape(row_total, HEADS, HEAD_DIM)
    )
    segment_row = segment_ids[0, 0]
    query_blocks = queries.reshape(block_total, block_rows, HEADS, HEAD_DIM)
    segment_blocks = segment_row.reshape(block_total, block_rows)

    def block_scores(query_block, query_segments):
        scores = (
            jnp.einsum("qhd,khd->hqk", query_block, key_heads, preferred_element_type=jnp.float32)
            * score_scale
        )
        allowed = query_segments[:, None] == segment_row[None, :]
        return jnp.where(allowed[None], scores, NEGATIVE)

    def attend(carried, pieces):
        scores = block_scores(pieces[0], pieces[1])
        row_max = jnp.max(scores, axis=-1, keepdims=True)
        exponent = jnp.exp(scores - row_max)
        row_sum = jnp.sum(exponent, axis=-1, keepdims=True)
        probability = (exponent / row_sum).astype(jnp.bfloat16)
        context_block = jnp.einsum(
            "hqk,khd->qhd", probability, value_heads, preferred_element_type=jnp.float32
        )
        return (carried, (context_block, (row_max + jnp.log(row_sum))[..., 0]))

    _, (contexts, logsums) = lax.scan(
        attend, jnp.zeros((), jnp.float32), (query_blocks, segment_blocks)
    )
    context = (
        (contexts.reshape(row_total, HEADS, HEAD_DIM) * head_keep[None, :, None])
        .reshape(row_total, width_model)
        .astype(jnp.bfloat16)
    )
    first_sum = mixed_rows + product(context, output_full) + output_bias_full
    normed, norm_first_back = jax.vjp(
        layer_norm, first_sum, gain_first.astype(jnp.float32), shift_first.astype(jnp.float32)
    )
    normed_low = normed.astype(jnp.bfloat16)
    inner_value = product(normed_low, inner_full) + inner_bias_full
    activated = (gelu_exact(inner_value) * unit_keep).astype(jnp.bfloat16)
    second_sum = normed + product(activated, outer_full) + outer_bias_full
    final, norm_second_back = jax.vjp(
        layer_norm, second_sum, gain_second.astype(jnp.float32), shift_second.astype(jnp.float32)
    )
    block_output = final.astype(jnp.bfloat16)[None]
    regathered = (
        lax.all_gather(query_weight, "dp", axis=0, tiled=True),
        lax.all_gather(key_weight, "dp", axis=0, tiled=True),
        lax.all_gather(value_weight, "dp", axis=0, tiled=True),
        lax.all_gather(output_weight, "dp", axis=0, tiled=True),
        lax.all_gather(inner_weight, "dp", axis=0, tiled=True),
        lax.all_gather(outer_weight, "dp", axis=0, tiled=True),
        lax.all_gather(query_bias, "dp", axis=0, tiled=True),
        lax.all_gather(value_bias, "dp", axis=0, tiled=True),
        lax.all_gather(output_bias, "dp", axis=0, tiled=True),
        lax.all_gather(inner_bias, "dp", axis=0, tiled=True),
        lax.all_gather(outer_bias, "dp", axis=0, tiled=True),
        lax.all_gather(attention_gain, "dp", axis=0, tiled=True),
        lax.all_gather(attention_shift, "dp", axis=0, tiled=True),
        lax.all_gather(feed_gain, "dp", axis=0, tiled=True),
        lax.all_gather(feed_shift, "dp", axis=0, tiled=True),
    )
    query_full, key_full, value_full, output_full, inner_full, outer_full = regathered[:6]
    second_grad, feed_gain_grad, feed_shift_grad = norm_second_back(
        cotangent[0].astype(jnp.float32)
    )
    outer_low = second_grad.astype(jnp.bfloat16)
    outer_bias_grad = column_sums(outer_low)
    outer_weight_grad = transposed_times(activated, outer_low)
    hidden_grad = times_transposed(outer_low, outer_full) * unit_keep
    _, gelu_back = jax.vjp(gelu_exact, inner_value)
    inner_low = gelu_back(hidden_grad)[0].astype(jnp.bfloat16)
    inner_bias_grad = column_sums(inner_low)
    inner_weight_grad = transposed_times(normed_low, inner_low)
    normed_grad = second_grad + times_transposed(inner_low, inner_full)
    first_grad, attention_gain_grad, attention_shift_grad = norm_first_back(normed_grad)
    attention_low = first_grad.astype(jnp.bfloat16)
    output_bias_grad = column_sums(attention_low)
    output_weight_grad = transposed_times(context, attention_low)
    context_grad = (
        times_transposed(attention_low, output_full).reshape(row_total, HEADS, HEAD_DIM)
        * head_keep[None, :, None]
    ).astype(jnp.bfloat16)
    context_blocks = context_grad.reshape(block_total, block_rows, HEADS, HEAD_DIM)

    def attend_back(carried, pieces):
        key_grad, value_grad = carried
        query_block, query_segments, logsum_block, context_block = pieces
        scores = block_scores(query_block, query_segments)
        probability = jnp.exp(scores - logsum_block[:, :, None])
        weights_low = probability.astype(jnp.bfloat16)
        value_grad = value_grad + jnp.einsum(
            "hqk,qhd->khd", weights_low, context_block, preferred_element_type=jnp.float32
        )
        prob_grad = jnp.einsum(
            "qhd,khd->hqk", context_block, value_heads, preferred_element_type=jnp.float32
        )
        score_grad = probability * (
            prob_grad - jnp.sum(probability * prob_grad, axis=-1, keepdims=True)
        )
        score_low = score_grad.astype(jnp.bfloat16)
        query_grad = (
            jnp.einsum("hqk,khd->qhd", score_low, key_heads, preferred_element_type=jnp.float32)
            * score_scale
        )
        key_grad = (
            key_grad
            + jnp.einsum("hqk,qhd->khd", score_low, query_block, preferred_element_type=jnp.float32)
            * score_scale
        )
        return ((key_grad, value_grad), query_grad.astype(jnp.bfloat16))

    empty_heads = jnp.zeros((row_total, HEADS, HEAD_DIM), jnp.float32)
    (key_total, value_total), query_grads = lax.scan(
        attend_back,
        (empty_heads, empty_heads),
        (query_blocks, segment_blocks, logsums, context_blocks),
    )
    query_low = query_grads.reshape(row_total, width_model)
    key_low = key_total.reshape(row_total, width_model).astype(jnp.bfloat16)
    value_low = value_total.reshape(row_total, width_model).astype(jnp.bfloat16)
    query_bias_grad = column_sums(query_low)
    value_bias_grad = column_sums(value_low)
    query_weight_grad = transposed_times(mixed_low, query_low)
    key_weight_grad = transposed_times(mixed_low, key_low)
    value_weight_grad = transposed_times(mixed_low, value_low)
    mixed_grad = (
        first_grad
        + times_transposed(query_low, query_full)
        + times_transposed(key_low, key_full)
        + times_transposed(value_low, value_full)
    )
    input_gradient = (
        jnp.zeros((row_total, width_model), jnp.float32).at[sources].add(mixed_grad)[None]
    )
    row_shards = (
        lax.psum_scatter(query_weight_grad, "dp", scatter_dimension=0, tiled=True),
        lax.psum_scatter(key_weight_grad, "dp", scatter_dimension=0, tiled=True),
        lax.psum_scatter(value_weight_grad, "dp", scatter_dimension=0, tiled=True),
        lax.psum_scatter(output_weight_grad, "dp", scatter_dimension=0, tiled=True),
        lax.psum_scatter(inner_weight_grad, "dp", scatter_dimension=0, tiled=True),
        lax.psum_scatter(outer_weight_grad, "dp", scatter_dimension=0, tiled=True),
        lax.psum_scatter(query_bias_grad, "dp", scatter_dimension=0, tiled=True),
        lax.psum_scatter(value_bias_grad, "dp", scatter_dimension=0, tiled=True),
        lax.psum_scatter(output_bias_grad, "dp", scatter_dimension=0, tiled=True),
        lax.psum_scatter(inner_bias_grad, "dp", scatter_dimension=0, tiled=True),
        lax.psum_scatter(outer_bias_grad, "dp", scatter_dimension=0, tiled=True),
        lax.psum_scatter(attention_gain_grad, "dp", scatter_dimension=0, tiled=True),
        lax.psum_scatter(attention_shift_grad, "dp", scatter_dimension=0, tiled=True),
        lax.psum_scatter(feed_gain_grad, "dp", scatter_dimension=0, tiled=True),
        lax.psum_scatter(feed_shift_grad, "dp", scatter_dimension=0, tiled=True),
    )
    (
        shard_query,
        shard_key,
        shard_value,
        shard_output,
        shard_inner,
        shard_outer,
        shard_query_bias,
        shard_value_bias,
        shard_output_bias,
        shard_inner_bias,
        shard_outer_bias,
        shard_first_gain,
        shard_first_shift,
        shard_second_gain,
        shard_second_shift,
    ) = row_shards
    totals = lax.psum(
        (
            shard_query,
            shard_key,
            shard_value,
            shard_output,
            shard_inner,
            shard_outer,
            shard_query_bias,
            shard_value_bias,
            shard_output_bias,
            shard_inner_bias,
            shard_outer_bias,
            shard_first_gain,
            shard_first_shift,
            shard_second_gain,
            shard_second_shift,
        ),
        "width",
    )
    return (block_output, input_gradient) + tuple(totals)


def solution(mesh):
    placed = (
        P("width", "dp", None),
        P("width", "dp", None),
        P("width", "dp"),
        P("width", "dp"),
        P("width", "dp", None),
        P("dp", None),
        P("dp", None),
        P("dp", None),
        P("dp", None),
        P("dp", None),
        P("dp", None),
        P("dp"),
        P("dp"),
        P("dp"),
        P("dp"),
        P("dp"),
        P("dp"),
        P("dp"),
        P("dp"),
        P("dp"),
    )
    return jax.shard_map(
        per_device,
        mesh=mesh,
        in_specs=placed,
        out_specs=(
            P("width", "dp", None),
            P("width", "dp", None),
            P("dp", None),
            P("dp", None),
            P("dp", None),
            P("dp", None),
            P("dp", None),
            P("dp", None),
            P("dp"),
            P("dp"),
            P("dp"),
            P("dp"),
            P("dp"),
            P("dp"),
            P("dp"),
            P("dp"),
            P("dp"),
        ),
        check_vma=False,
    )
```

profile of v0, /device:TPU:0, one launch (start us, length us, event | category | flops | bytes accessed | tf_op | source)
XLA Modules:
  0.0 1221.6 jit_solution(11421575083259113259)
XLA Ops:
  21.3 38.9 %all-reduce.20 = (bf16[768]{0:T(1024)(128)(2,1)S(1)}, bf16[768]{0:T(1024)(128)(2,1)S(1)}, bf16[768]{0:T(1024)(128)(2,1)S(1)}, bf16[768]{0:T(1024)(128)(2,1)S(1)}...) all-reduce(bf16[768]{0:T(1024)(128)(2,1)S(1)} %dynamic-update-slice, ...), channel_id=1, replica_groups=mesh['width'=4,'dp'=8] {'dp'}, use_global_device_ids=true, to_apply=%add.2 | all-reduce | flops 6144 | bytes 24576
  67.7 26.0 %all-gather = bf16[8,1,384]{2,1,0:T(2,128)(2,1)S(1)} all-gather(bf16[1,1,384]{2,1,0:T(2,128)(2,1)S(1)} %reshape.317), channel_id=1, replica_groups=mesh['width'=4,'dp'=8] {'dp'}, dimensions={0}, use_global_device_ids=true | all-gather | bytes 6912 | tf_op jit(solution)/shard_map/all_gather | solution.py:78
  114.0 24.5 %all-gather.12.cloned.1.call-done = bf16[768,768]{1,0:T(8,128)(2,1)} async-done(((bf16[96,768]{1,0:T(8,128)(2,1)}), bf16[768,768]{1,0:T(8,128)(2,1)}) %all-gather.12.cloned.1.call-update) | async-done | bytes 1179664 | tf_op jit(solution)/shard_map/all_gather | solution.py:71
  142.3 135.8 %while.27 = (s32[]{:T(128)}, f32[2,512,12,64]{1,0,3,2:T(2,128)}, f32[2,12,512]{2,1,0:T(8,128)S(1)}, s32[2,512]{1,0:T(2,128)S(1)}, s32[1,1,1024]{2,1,0:T(1,128)S(...) while((s32[]{:T(128)}, f32[2,512,12,64]{1,0,3,2:T(2,128)}, ...), condition=%wide.region_3.4_spmd, body=%wide.region_0.3_spmd.sunk | while | flops 1686628352 | bytes 190285984 | solution.py:147
  155.1 12.4 %fusion.129 = f32[12,512]{1,0:T(8,128)S(1)} fusion(f32[12,512,1024]{2,1,0:T(8,128)} %get-tuple-element.481, f32[12,512]{1,0:T(8,128)S(1)} %get-tuple-element.482, pred[512,1024]{1,0:T(8,128)(4,1)S(1)} %broadcast_compare_fusion.4), kind=kLoop, calls=%fused_computation.6.clone.1 | loop fusion | flops 25159680 | bytes 25739264 | tf_op jit(solution)/shard_map/while/body/eval_jaxpr/reduce_sum | solution.py:140
  181.4 28.9 %dynamic_update_slice.19 = f32[2,512,12,64]{1,0,3,2:T(2,128)} dynamic-update-slice(f32[2,512,12,64]{1,0,3,2:T(2,128)} %get-tuple-element.507, f32[1,512,12,64]{1,0,3,2:T(1,128)S(1)} %copy.104, s32[]{:T(128)S(6)} %copy.119, s32[]{:T(128)} %constant.72.clone.1..sunk, s32[]{:T(128)} %constant.72.clone.1..sunk, s32[]{:T(128)} %constant.72.clone.1..sunk) | dynamic-update-slice | bytes 3145732 | tf_op jit(solution)/shard_map/while/body/jit(dynamic_update_index_in_dim)/dynamic_update_slice | solution.py:147
  222.9 12.4 %fusion.129 = f32[12,512]{1,0:T(8,128)S(1)} fusion(f32[12,512,1024]{2,1,0:T(8,128)} %get-tuple-element.481, f32[12,512]{1,0:T(8,128)S(1)} %get-tuple-element.482, pred[512,1024]{1,0:T(8,128)(4,1)S(1)} %broadcast_compare_fusion.4), kind=kLoop, calls=%fused_computation.6.clone.1 | loop fusion | flops 25159680 | bytes 25739264 | tf_op jit(solution)/shard_map/while/body/eval_jaxpr/reduce_sum | solution.py:140
  249.1 28.9 %dynamic_update_slice.19 = f32[2,512,12,64]{1,0,3,2:T(2,128)} dynamic-update-slice(f32[2,512,12,64]{1,0,3,2:T(2,128)} %get-tuple-element.507, f32[1,512,12,64]{1,0,3,2:T(1,128)S(1)} %copy.104, s32[]{:T(128)S(6)} %copy.119, s32[]{:T(128)} %constant.72.clone.1..sunk, s32[]{:T(128)} %constant.72.clone.1..sunk, s32[]{:T(128)} %constant.72.clone.1..sunk) | dynamic-update-slice | bytes 3145732 | tf_op jit(solution)/shard_map/while/body/jit(dynamic_update_index_in_dim)/dynamic_update_slice | solution.py:147
  289.3 38.3 %multiply_convert_fusion.2 = (bf16[1024,3072]{1,0:T(8,128)(2,1)}, f32[1024,3072]{1,0:T(8,128)}, f32[1024,3072]{1,0:T(8,128)}) fusion(f32[3072]{0:T(1024)S(1)} %copy-done.52, f32[3072]{0:T(1024)S(1)} %bitcast.191, bf16[768,3072]{1,0:T(8,128)(2,1)} %all-gather.16.cloned.1.call-done, f32[1024,768]{0,1:T(8,128)} %copy-done.10, f32[768]{0:T(1024)S(1)} %copy-done.56, ...), kind=kOutput, calls=%fused_computation.52 | convolution fusion | flops 5046534144 | bytes 39360512 | tf_op jit(solution)/shard_map/dot_general | solution.py:27
  327.6 13.5 %all-gather.18.cloned.1.call-done = bf16[3072,768]{1,0:T(8,128)(2,1)} async-done(((bf16[384,768]{1,0:T(8,128)(2,1)}), bf16[3072,768]{1,0:T(8,128)(2,1)}) %all-gather.18.cloned.1.call-update) | async-done | bytes 4718608 | tf_op jit(solution)/shard_map/all_gather | solution.py:74
  357.3 18.7 %convert_reduce_fusion = (f32[3072]{0:T(1024)}, bf16[1024,3072]{1,0:T(8,128)(2,1)}) fusion(f32[1024,3072]{1,0:T(8,128)} %get-tuple-element.354, f32[3072]{0:T(1024)S(1)} %copy-done.52, bf16[1024,768]{0,1:T(8,128)(2,1)S(1)} %get-tuple-element.346, bf16[3072,768]{1,0:T(8,128)(2,1)} %all-gather.18.cloned.1.call-done, f32[1024,3072]{1,0:T(8,128)} %get-tuple-element.366, ...), kind=kOutput, calls=%fused_computation.50 | convolution fusion | flops 4888458240 | bytes 37785600 | tf_op jit(solution)/shard_map/dot_general | solution.py:37
  408.3 169.4 %while.28 = (s32[]{:T(128)}, f32[1024,12,64]{0,2,1:T(8,128)}, f32[1024,12,64]{0,2,1:T(8,128)}, bf16[2,512,12,64]{1,3,2,0:T(8,128)(2,1)}, bf16[2,512,12,64]{1,3,2...) while((s32[]{:T(128)}, f32[1024,12,64]{0,2,1:T(8,128)}, ...), condition=%wide.region_14.15_spmd.clone, body=%wide.region_12.14_spmd.clone.sunk | while | flops 4126140416 | bytes 218556592 | solution.py:235
  420.5 13.7 %bitcast_add_fusion.5 = f32[1024,12,64]{0,2,1:T(8,128)} fusion(f32[1024,12,64]{0,2,1:T(8,128)} %get-tuple-element.541, f32[12,512,1024]{2,1,0:T(8,128)} %fusion.140, f32[12,512]{1,0:T(8,128)S(1)} %dynamic-slice_bitcast_fusion.2, pred[512,1024]{1,0:T(8,128)(4,1)S(1)} %broadcast_compare_fusion.5, pred[]{:T(512)S(6)} %compare.7, ...), kind=kOutput, calls=%fused_computation.24.clone.1 | convolution fusion | flops 832045056 | bytes 32800772 | tf_op jit(solution)/shard_map/while/body/eval_jaxpr/hqk,qhd->khd/dot_general | solution.py:213
  434.3 18.2 %multiply_reduce_fusion.6 = (f32[12,512]{1,0:T(8,128)S(1)}, f32[12,512,1024]{2,1,0:T(8,128)}) fusion(f32[12,512,1024]{2,1,0:T(8,128)} %fusion.140, f32[12,512]{1,0:T(8,128)S(1)} %dynamic-slice_bitcast_fusion.2, pred[512,1024]{1,0:T(8,128)(4,1)S(1)} %broadcast_compare_fusion.5, bf16[1024,12,64]{0,2,1:T(8,128)(2,1)} %get-tuple-element.562, ...), kind=kOutput, calls=%fused_computation.19.clone.1 | convolution fusion | flops 836757504 | bytes 53264388 | tf_op jit(solution)/shard_map/while/body/eval_jaxpr/qhd,khd->hqk/dot_general | solution.py:216
  452.5 22.0 %multiply_convert_fusion.8 = bf16[12,512,1024]{2,1,0:T(8,128)(2,1)} fusion(f32[12,512,1024]{2,1,0:T(8,128)} %get-tuple-element.494, f32[12,512,1024]{2,1,0:T(8,128)} %fusion.140, f32[12,512]{1,0:T(8,128)S(1)} %get-tuple-element.495, f32[12,512]{1,0:T(8,128)S(1)} %dynamic-slice_bitcast_fusion.2, pred[512,1024]{1,0:T(8,128)(4,1)S(1)} %broadcast_compare_fusion.5), kind=kLoop, calls=%fused_computation.18.clone.1 | loop fusion | flops 37748736 | bytes 63488000 | tf_op jit(solution)/shard_map/while/body/eval_jaxpr/convert_element_type | solution.py:222
  504.6 14.3 %bitcast_add_fusion.5 = f32[1024,12,64]{0,2,1:T(8,128)} fusion(f32[1024,12,64]{0,2,1:T(8,128)} %get-tuple-element.541, f32[12,512,1024]{2,1,0:T(8,128)} %fusion.140, f32[12,512]{1,0:T(8,128)S(1)} %dynamic-slice_bitcast_fusion.2, pred[512,1024]{1,0:T(8,128)(4,1)S(1)} %broadcast_compare_fusion.5, pred[]{:T(512)S(6)} %compare.7, ...), kind=kOutput, calls=%fused_computation.24.clone.1 | convolution fusion | flops 832045056 | bytes 32800772 | tf_op jit(solution)/shard_map/while/body/eval_jaxpr/hqk,qhd->khd/dot_general | solution.py:213
  518.9 18.1 %multiply_reduce_fusion.6 = (f32[12,512]{1,0:T(8,128)S(1)}, f32[12,512,1024]{2,1,0:T(8,128)}) fusion(f32[12,512,1024]{2,1,0:T(8,128)} %fusion.140, f32[12,512]{1,0:T(8,128)S(1)} %dynamic-slice_bitcast_fusion.2, pred[512,1024]{1,0:T(8,128)(4,1)S(1)} %broadcast_compare_fusion.5, bf16[1024,12,64]{0,2,1:T(8,128)(2,1)} %get-tuple-element.562, ...), kind=kOutput, calls=%fused_computation.19.clone.1 | convolution fusion | flops 836757504 | bytes 53264388 | tf_op jit(solution)/shard_map/while/body/eval_jaxpr/qhd,khd->hqk/dot_general | solution.py:216
  537.1 21.2 %multiply_convert_fusion.8 = bf16[12,512,1024]{2,1,0:T(8,128)(2,1)} fusion(f32[12,512,1024]{2,1,0:T(8,128)} %get-tuple-element.494, f32[12,512,1024]{2,1,0:T(8,128)} %fusion.140, f32[12,512]{1,0:T(8,128)S(1)} %get-tuple-element.495, f32[12,512]{1,0:T(8,128)S(1)} %dynamic-slice_bitcast_fusion.2, pred[512,1024]{1,0:T(8,128)(4,1)S(1)} %broadcast_compare_fusion.5), kind=kLoop, calls=%fused_computation.18.clone.1 | loop fusion | flops 37748736 | bytes 63488000 | tf_op jit(solution)/shard_map/while/body/eval_jaxpr/convert_element_type | solution.py:222
  618.1 34.6 %reduce-scatter.7.cloned.1.call-done = f32[96,768]{1,0:T(8,128)} async-done(((f32[768,768]{1,0:T(8,128)}), f32[96,768]{1,0:T(8,128)}) %reduce-scatter.7.cloned.1.call-update) | async-done | bytes 294928 | tf_op jit(solution)/shard_map/reduce_scatter | solution.py:258
  652.7 71.5 %reduce-scatter.9.cloned.1.call-done = f32[96,768]{1,0:T(8,128)} async-done(((f32[768,768]{1,0:T(8,128)}), f32[96,768]{1,0:T(8,128)}) %reduce-scatter.9.cloned.1.call-update) | async-done | bytes 294928 | tf_op jit(solution)/shard_map/reduce_scatter | solution.py:259
  724.2 71.4 %reduce-scatter.11.cloned.1.call-done = f32[96,768]{1,0:T(8,128)} async-done(((f32[768,768]{1,0:T(8,128)}), f32[96,768]{1,0:T(8,128)}) %reduce-scatter.11.cloned.1.call-update) | async-done | bytes 294928 | tf_op jit(solution)/shard_map/reduce_scatter | solution.py:260
  795.6 166.1 %reduce-scatter.15.cloned.1.call-done = f32[96,3072]{1,0:T(8,128)} async-done(((f32[768,3072]{1,0:T(8,128)}), f32[96,3072]{1,0:T(8,128)}) %reduce-scatter.15.cloned.1.call-update) | async-done | bytes 1179664 | tf_op jit(solution)/shard_map/reduce_scatter | solution.py:262
  961.7 166.0 %reduce-scatter.17.cloned.1.call-done = f32[384,768]{1,0:T(8,128)} async-done(((f32[3072,768]{1,0:T(8,128)}), f32[384,768]{1,0:T(8,128)}) %reduce-scatter.17.cloned.1.call-update) | async-done | bytes 1179664 | tf_op jit(solution)/shard_map/reduce_scatter | solution.py:263
  1132.7 35.9 %all-reduce.17 = (f32[768]{0:T(1024)S(1)}, f32[768]{0:T(1024)S(1)}, f32[768]{0:T(1024)S(1)}, f32[3072]{0:T(1024)S(1)}, f32[768]{0:T(1024)S(1)}, /*index=5*/f32[7...) all-reduce(f32[768]{0:T(1024)S(1)} %reduce_sum.216, ...), channel_id=8, replica_groups=mesh['width'=4,'dp'=8] {'dp'}, use_global_device_ids=true, to_apply=%region_29.30.clone | all-reduce | flops 9216 | bytes 73728
  (306 shorter events, 306.9 us)
Async XLA Ops:
  7.2 87.8 %copy-start = (bf16[1,1024,768]{2,1,0:T(8,128)(2,1)S(1)}, bf16[1,1024,768]{2,1,0:T(8,128)(2,1)}, u32[]{:S(2)}) copy-start(bf16[1,1024,768]{2,1,0:T(8,128)(2,1)} %param.24) | copy-start | bytes 4718596
  7.2 95.1 %all-gather.8.cloned.1.call-start = ((), (), s32[]{:S(2)}) async-start(), calls=%async_computation.6 | async-start | bytes 1327104 | tf_op jit(solution)/shard_map/all_gather | solution.py:69
  7.9 102.7 %all-gather.10.cloned.1.call-start = ((), (), s32[]{:S(2)}) async-start(), calls=%async_computation.7 | async-start | bytes 1327104 | tf_op jit(solution)/shard_map/all_gather | solution.py:70
  8.7 129.7 %all-gather.12.cloned.1.call-start = ((), (), s32[]{:S(2)}) async-start(), calls=%async_computation.8 | async-start | bytes 1327104 | tf_op jit(solution)/shard_map/all_gather | solution.py:71
  9.4 273.7 %all-gather.14.cloned.1.call-start = ((), (), s32[]{:S(2)}) async-start(), calls=%async_computation.9 | async-start | bytes 1327104 | tf_op jit(solution)/shard_map/all_gather | solution.py:72
  10.0 279.3 %all-gather.16.cloned.1.call-start = ((), (), s32[]{:S(2)}) async-start(), calls=%async_computation.10 | async-start | bytes 5308416 | tf_op jit(solution)/shard_map/all_gather | solution.py:73
  10.6 330.6 %all-gather.18.cloned.1.call-start = ((), (), s32[]{:S(2)}) async-start(), calls=%async_computation.11 | async-start | bytes 5308416 | tf_op jit(solution)/shard_map/all_gather | solution.py:74
  11.2 607.0 %reduce-scatter.13.cloned.1.call-start = ((), (), s32[]{:S(2)}) async-start(), calls=%async_computation.15 | async-start | bytes 2654208 | tf_op jit(solution)/shard_map/reduce_scatter | solution.py:261
  11.9 83.0 %copy-start.62 = (f32[12]{0:T(128)}, f32[12]{0:T(128)S(1)}, u32[]{:S(2)}) copy-start(f32[12]{0:T(128)S(1)} %compare_convert_fusion) | copy-start | bytes 148
  102.3 36.1 %copy-start.64 = (pred[1024]{0:T(1024)(128)(4,1)}, pred[1024]{0:T(1024)(128)(4,1)S(1)}, u32[]{:S(2)}) copy-start(pred[1024]{0:T(1024)(128)(4,1)S(1)} %compare_and_fusion) | copy-start | bytes 3076
  110.7 27.8 %copy-start.18 = (bf16[1024,768]{0,1:T(8,128)(2,1)S(1)}, bf16[1024,768]{0,1:T(8,128)(2,1)}, u32[]{:S(2)}) copy-start(bf16[1024,768]{0,1:T(8,128)(2,1)} %copy.62) | copy-start | bytes 4718596
  114.0 28.4 %copy-start.30 = (s32[1,1,1024]{2,1,0:T(1,128)S(1)}, s32[1,1,1024]{2,1,0:T(1,128)}, u32[]{:S(2)}) copy-start(s32[1,1,1024]{2,1,0:T(1,128)} %param.28) | copy-start | bytes 12292
  287.3 100.6 %copy-start.39 = (f32[1024]{0:T(1024)}, f32[1024]{0:T(1024)S(1)}, u32[]{:S(2)}) copy-start(f32[1024]{0:T(1024)S(1)} %broadcast_multiply_fusion.1) | copy-start | bytes 12292
  289.3 98.6 %copy-start.43 = (f32[1024]{0:T(1024)}, f32[1024]{0:T(1024)S(1)}, u32[]{:S(2)}) copy-start(f32[1024]{0:T(1024)S(1)} %fusion.54) | copy-start | bytes 12292
  289.3 51.8 %copy-start.58 = (f32[768]{0:T(1024)S(1)}, f32[768]{0:T(1024)}, u32[]{:S(2)}) copy-start(f32[768]{0:T(1024)} %convert_element_type.144) | copy-start | bytes 9220
  357.3 18.7 %copy-start.23 = (bf16[1024,768]{0,1:T(8,128)(2,1)}, bf16[1024,768]{0,1:T(8,128)(2,1)S(1)}, u32[]{:S(2)}) copy-start(bf16[1024,768]{0,1:T(8,128)(2,1)S(1)} %get-tuple-element.346) | copy-start | bytes 4718596
  394.6 258.1 %reduce-scatter.7.cloned.1.call-start = ((), (), s32[]{:S(2)}) async-start(), calls=%async_computation.12 | async-start | bytes 2654208 | tf_op jit(solution)/shard_map/reduce_scatter | solution.py:258
  585.4 138.8 %reduce-scatter.9.cloned.1.call-start = ((), (), s32[]{:S(2)}) async-start(), calls=%async_computation.13 | async-start | bytes 2654208 | tf_op jit(solution)/shard_map/reduce_scatter | solution.py:259
  590.5 205.1 %reduce-scatter.11.cloned.1.call-start = ((), (), s32[]{:S(2)}) async-start(), calls=%async_computation.14 | async-start | bytes 2654208 | tf_op jit(solution)/shard_map/reduce_scatter | solution.py:260
  595.6 366.1 %reduce-scatter.15.cloned.1.call-start = ((), (), s32[]{:S(2)}) async-start(), calls=%async_computation.16 | async-start | bytes 10616832 | tf_op jit(solution)/shard_map/reduce_scatter | solution.py:262
  606.4 521.3 %reduce-scatter.17.cloned.1.call-start = ((), (), s32[]{:S(2)}) async-start(), calls=%async_computation.17 | async-start | bytes 10616832 | tf_op jit(solution)/shard_map/reduce_scatter | solution.py:263
  618.1 509.7 %copy-start.6 = (bf16[1,1024,768]{1,2,0:T(8,128)(2,1)S(1)}, bf16[1,1024,768]{1,2,0:T(8,128)(2,1)}, u32[]{:S(2)}) copy-start(bf16[1,1024,768]{1,2,0:T(8,128)(2,1)} %copy.66) | copy-start | bytes 4718596
  618.1 587.6 %all-reduce.23.cloned.1.call-start = ((), (), s32[]{:S(2)}) async-start(), calls=%async_computation.18 | async-start | bytes 7077888 | tf_op jit(solution)/shard_map/psum | solution.py:291
  1128.1 41.1 %copy-start.22 = (bf16[96,8,2,512]{3,1,2,0:T(8,128)(2,1)S(1)}, bf16[96,8,2,512]{3,1,2,0:T(8,128)(2,1)}, u32[]{:S(2)}) copy-start(bf16[96,8,2,512]{3,1,2,0:T(8,128)(2,1)} %copy-done.21) | copy-start | bytes 4718596
  (60 other events, 282.5 us)
Sparse Core Ops, SparseCore 0:
  10.2 44.0 all-gather.7
  56.5 39.7 all-gather.9
  98.6 39.8 all-gather.11
  140.5 39.8 all-gather.13
  182.4 78.6 all-gather.15
  263.1 78.0 all-gather.17
  394.7 67.1 reduce-scatter.12
  585.5 67.1 reduce-scatter.6
  656.2 67.9 reduce-scatter.8
  727.5 68.0 reduce-scatter.10
  799.2 162.4 reduce-scatter.14
  965.2 162.5 reduce-scatter.16
  1130.5 75.1 all-reduce.22
where the time goes:
time: 1230 us; the launch traced here: 1220 us
  waiting for transfers between devices  559 us (45%)
  matrix products  304 us (25%)
  local copies, waits for them, and re-layouts  129 us (10%)
  blocking collectives  108 us (9%)
  other arithmetic  103 us (8%)
  between operations  18.1 us (1%)
    reduce_scatter x1, waiting for transfers between devices, per_device(): lax.psum_scatter(inner_weight_grad, 'dp', scatter_dimension=0, tiled=True)  166 us
    reduce_scatter x1, waiting for transfers between devices, per_device(): lax.psum_scatter(outer_weight_grad, 'dp', scatter_dimension=0, tiled=True)  166 us
    unnamed x2, blocking collectives  74.9 us
    reduce_scatter x1, waiting for transfers between devices, per_device(): lax.psum_scatter(key_weight_grad, 'dp', scatter_dimension=0, tiled=True)  71.5 us
    reduce_scatter x1, waiting for transfers between devices, per_device(): lax.psum_scatter(value_weight_grad, 'dp', scatter_dimension=0, tiled=True)  71.4 us
    dot_general x6, matrix products, product(): return jnp.dot(matrix, second, preferred_element_type=jnp.float32)  63 us
    dynamic_update_slice x4, local copies, waits for them, and re-layouts, per_device(): lax.scan(attend, jnp.zeros((), jnp.float32), (query_blocks, segment_blocks))  60.9 us
    dot_general x4, matrix products, block_scores(): jnp.einsum('qhd,khd->hqk', query_block, key_heads, preferred_element_type...  47.3 us
  transfers between devices with their start and end apart: 13, of which 8 were waited for; matrix products, arithmetic and copies ran while one was open for 38% of the time, Pallas kernels for 0%

commit v1 on v0

v1 whole, which is shorter than its diff:
```python
import functools

import jax
import jax.numpy as jnp
from jax import lax
from jax.experimental import pallas as pl
from jax.experimental.pallas import tpu as pltpu
from jax.sharding import PartitionSpec as P

HEADS = 12
HEAD_DIM = 64
EPSILON = 1e-12
NEGATIVE = -1000000000.0
QB = 256
PIECES = 8
WIDTHS = 4
bf16 = jnp.bfloat16
f32 = jnp.float32
MIB = 2**20
NN = (((1,), (0,)), ((), ()))
NT = (((1,), (1,)), ((), ()))
TN = (((0,), (0,)), ((), ()))
SMEM = pl.BlockSpec(memory_space=pltpu.SMEM)
ANY = pl.BlockSpec(memory_space=pl.ANY)


def dot(a, b, dims=NN):
    return lax.dot_general(a, b, dims, preferred_element_type=f32)


def params(mib):
    return pltpu.CompilerParams(vmem_limit_bytes=mib * MIB)


def cost(flops, moved, transcendentals=0):
    return pl.CostEstimate(flops=flops, bytes_accessed=moved, transcendentals=transcendentals)


def whole(shape):
    return pl.BlockSpec(shape, lambda *_: (0,) * len(shape))


def shape_of(shape, kind=bf16):
    return jax.ShapeDtypeStruct(shape, kind)


def slot_of(piece, home):
    return ((piece & 1) ^ (home & 1)) * 4 + ((piece >> 1) ^ (home >> 1))


def mix_kernel(src_ref, x_ref, mixed_ref):
    rows, total = src_ref.shape[0], x_ref.shape[0]
    pick = src_ref[...] == lax.broadcasted_iota(jnp.int32, (rows, total), 1)
    mixed_ref[...] = dot(jnp.where(pick, 1.0, 0.0).astype(bf16), x_ref[...]).astype(bf16)


def mix(src_col, x):
    total, width = x.shape
    return pl.pallas_call(
        mix_kernel,
        in_specs=[whole((total, 1)), whole((total, width))],
        out_specs=whole((total, width)),
        out_shape=shape_of((total, width)),
        compiler_params=params(24),
        cost_estimate=cost(2 * total * total * width, 4 * total * width),
        name="mix",
    )(src_col, x)


def fetch_halves(sc, sources, weights, sem):
    rows = weights.shape[1] // PIECES
    for other, source in enumerate(sources):
        half = (sc[0] & 1) ^ other
        for piece in range(PIECES):
            pltpu.make_async_copy(
                source.at[slot_of(piece, sc[1]), pl.ds(0, rows), :],
                weights.at[half, pl.ds(piece * rows, rows), :],
                sem,
            ).start()


def project_kernel(sc, mixed_ref, bias_ref, own, other, q_ref, k_ref, v_ref, weights, sem):
    part = weights.shape[2] // 3

    @pl.when(pl.program_id(0) == 0)
    def _():
        fetch_halves(sc, (own, other), weights, sem)
        pltpu.make_async_copy(weights, weights, sem).wait()

    for half in range(2):
        out = dot(mixed_ref[...], weights[half]) + bias_ref[half : half + 1, :].astype(f32)
        here = slice(half * part, (half + 1) * part)
        q_ref[:, here] = out[:, :part].astype(bf16) * jnp.asarray(HEAD_DIM**-0.5, bf16)
        k_ref[:, here] = out[:, part : 2 * part].astype(bf16)
        v_ref[:, here] = out[:, 2 * part :].astype(bf16)


def project(sc, mixed, bias, own, other, tile=512):
    total, width = mixed.shape
    columns = own.shape[2]
    rows = pl.BlockSpec((tile, width), lambda i: (i, 0))
    return pl.pallas_call(
        project_kernel,
        grid=(total // tile,),
        in_specs=[SMEM, rows, whole(bias.shape), ANY, ANY],
        out_specs=[rows] * 3,
        out_shape=[shape_of((total, width))] * 3,
        scratch_shapes=[pltpu.VMEM((2, width, columns), bf16), pltpu.SemaphoreType.DMA],
        compiler_params=params(40),
        cost_estimate=cost(4 * total * width * columns, 12 * total * width),
        name="project",
    )(sc, mixed, bias, own, other)


def keep_lanes(value, head):
    lane = lax.broadcasted_iota(jnp.int32, value.shape, 1)
    return jnp.where(lane // HEAD_DIM == head, value, jnp.zeros_like(value))


def for_window(windows, block, total, run):
    start = pl.multiple_of(windows[0, block], 128)
    need = windows[1, block]
    for size in range(QB, total + 1, QB):

        @pl.when(need == size)
        def _():
            run(start, size)


def attend_kernel(sc, windows, seg_col, seg_row, q_ref, k_ref, v_ref, ctx_ref, lse_ref, vt_ref):
    total = q_ref.shape[0]
    left = sc[3] - 2 * pl.program_id(0)

    @pl.when(left <= 0)
    def _():
        ctx_ref[...] = jnp.zeros_like(ctx_ref)
        lse_ref[...] = jnp.zeros_like(lse_ref)

    @pl.when(left > 0)
    def _():
        vt_ref[...] = v_ref[...].T
        for block in range(total // QB):

            def run(start, size, block=block):
                here = pl.ds(block * QB, QB)
                keys = k_ref[pl.ds(start, size), :]
                queries = q_ref[here, :]
                allowed = seg_col[pl.ds(start, size), :] == seg_row[:, here]
                parts = []
                for head in range(2):
                    s = dot(keys, keep_lanes(queries, head), NT)
                    s = jnp.where(allowed, s, NEGATIVE)
                    top = jnp.max(s, axis=0, keepdims=True)
                    e = jnp.exp(s - top)
                    norm = jnp.sum(e, axis=0, keepdims=True)
                    values = vt_ref[head * HEAD_DIM : (head + 1) * HEAD_DIM, pl.ds(start, size)]
                    parts.append(dot(values, e.astype(bf16)) * (1.0 / norm))
                    lse_ref[0, head : head + 1, here] = top + jnp.log(norm)
                both = jnp.concatenate(parts, axis=0).T
                lane = lax.broadcasted_iota(jnp.int32, both.shape, 1)
                ctx_ref[here, :] = jnp.where(lane < left * HEAD_DIM, both, 0.0).astype(bf16)

            for_window(windows, block, total, run)


def attend(sc, windows, seg_col, seg_row, q, k, v):
    total, width = q.shape
    pairs = width // 128
    cols = pl.BlockSpec((total, 128), lambda i: (0, i))
    return pl.pallas_call(
        attend_kernel,
        grid=(pairs,),
        in_specs=[SMEM, SMEM, whole(seg_col.shape), whole(seg_row.shape), cols, cols, cols],
        out_specs=[cols, pl.BlockSpec((1, 2, total), lambda i: (i, 0, 0))],
        out_shape=[shape_of((total, width)), shape_of((pairs, 2, total), f32)],
        scratch_shapes=[pltpu.VMEM((128, total), bf16)],
        compiler_params=params(40),
        cost_estimate=cost(16 * total * total * width, 8 * total * width, total * total * HEADS),
        name="attend",
    )(sc, windows, seg_col, seg_row, q, k, v)


def attend_back_kernel(
    first, sc, windows, seg_col, seg_row, q_ref, k_ref, v_ref, c_ref, lse_ref,
    dq_ref, dk_ref, dv_ref, kt_ref, dk_sum, dv_sum,
):
    total = q_ref.shape[0]
    left = sc[3] - 2 * (pl.program_id(0) + first)

    @pl.when(left <= 0)
    def _():
        for ref in (dq_ref, dk_ref, dv_ref):
            ref[...] = jnp.zeros_like(ref)

    @pl.when(left > 0)
    def _():
        kt_ref[...] = k_ref[...].T
        dk_sum[...] = jnp.zeros_like(dk_sum)
        dv_sum[...] = jnp.zeros_like(dv_sum)
        for block in range(total // QB):

            def run(start, size, block=block):
                here = pl.ds(block * QB, QB)
                there = pl.ds(start, size)
                keys = k_ref[there, :]
                values = v_ref[there, :]
                allowed = seg_col[there, :] == seg_row[:, here]
                qs = [keep_lanes(q_ref[here, :], head) for head in range(2)]
                cs = [keep_lanes(c_ref[here, :], head) for head in range(2)]
                dq, weights, scores = [], [], []
                for head in range(2):
                    s = dot(keys, qs[head], NT)
                    dp = dot(values, cs[head], NT)
                    p = jnp.where(allowed, jnp.exp(s - lse_ref[0, head : head + 1, here]), 0.0)
                    t = p * dp
                    ds = (t - p * jnp.sum(t, axis=0, keepdims=True)).astype(bf16)
                    weights.append(p.astype(bf16))
                    scores.append(ds)
                    dq.append(dot(kt_ref[head * HEAD_DIM : (head + 1) * HEAD_DIM, there], ds))
                dv_sum[there, :] += dot(weights[0], cs[0]) + dot(weights[1], cs[1])
                dk_sum[there, :] += dot(scores[0], qs[0]) + dot(scores[1], qs[1])
                both = jnp.concatenate(dq, axis=0).T
                dq_ref[here, :] = (both * HEAD_DIM**-0.5).astype(bf16)

            for_window(windows, block, total, run)
        dk_ref[...] = dk_sum[...].astype(bf16)
        dv_ref[...] = dv_sum[...].astype(bf16)


def attend_back(half, sc, windows, seg_col, seg_row, q, k, v, c, lse):
    total, width = q.shape
    pairs = width // 256
    first = half * pairs
    cols = pl.BlockSpec((total, 128), lambda i: (0, i + first))
    return pl.pallas_call(
        functools.partial(attend_back_kernel, first),
        grid=(pairs,),
        in_specs=[SMEM, SMEM, whole(seg_col.shape), whole(seg_row.shape), cols, cols, cols, cols,
                  pl.BlockSpec((1, 2, total), lambda i: (i + first, 0, 0))],
        out_specs=[pl.BlockSpec((total, 128), lambda i: (0, i))] * 3,
        out_shape=[shape_of((total, width // 2))] * 3,
        scratch_shapes=[
            pltpu.VMEM((128, total), bf16),
            pltpu.VMEM((total, 128), f32),
            pltpu.VMEM((total, 128), f32),
        ],
        compiler_params=params(48),
        cost_estimate=cost(20 * total * total * width, 8 * total * width, total * total * HEADS // 2),
        name="attend_back",
    )(sc, windows, seg_col, seg_row, q, k, v, c, lse)


def row_mean(value):
    return jnp.mean(value, axis=1, keepdims=True)


def normalise(hidden):
    centred = hidden - row_mean(hidden)
    rate = lax.rsqrt(row_mean(centred * centred) + EPSILON)
    return centred * rate, rate


def norm_back(grad, gain, unit, rate):
    scaled = grad * gain
    return rate * (scaled - row_mean(scaled) - unit * row_mean(scaled * unit))


def col_sum(value):
    return jnp.sum(value, axis=0, keepdims=True)


def feed_kernel(
    sc, mixed_ref, ctx_ref, cot_ref, bi_ref, vec_ref, f0, f1, f2, f3,
    out_ref, first_ref, dctx_ref, dwo_ref, dbi_ref, sums_ref, keep_i, send_i, keep_u, send_u,
    wi, wu, wo, act, slope, unit_ref, grad_ref, low_ref, glow_ref, rate_ref, stage,
    wo_sem, wi_sem, wu_sem, out_sem,
):
    total, width = mixed_ref.shape
    unit_rows = width // PIECES
    outer_rows = wi.shape[0] * width // PIECES
    own, home, active, heads = sc[0], sc[1], sc[2], sc[3]
    sources = (f0, f1, f2, f3)
    ob, g1, s1, ub, g2, s2 = (vec_ref[i : i + 1, :].astype(f32) for i in range(6))

    half_rows = unit_rows // 2
    for slot in range(2):
        for piece in range(PIECES):
            at = pl.multiple_of(piece * unit_rows + ((own & 1) ^ slot) * half_rows, 16)
            pltpu.make_async_copy(
                sources[slot].at[slot_of(piece, home), pl.ds(2 * unit_rows, half_rows), :],
                wo.at[pl.ds(at, half_rows), :],
                wo_sem,
            ).start()
    for slot in range(WIDTHS):
        for piece in range(PIECES):
            pltpu.make_async_copy(
                sources[slot].at[slot_of(piece, home), pl.ds(0, unit_rows), :],
                wi.at[slot, pl.ds(piece * unit_rows, unit_rows), :],
                wi_sem.at[slot],
            ).start()
        for end in range(2):
            for part in range(WIDTHS):
                at = pl.multiple_of(end * outer_rows + (own ^ part) * unit_rows, 16)
                pltpu.make_async_copy(
                    sources[part].at[slot_of(2 * (own ^ slot) + end, home), pl.ds(unit_rows, unit_rows), :],
                    wu.at[slot, pl.ds(at, unit_rows), :],
                    wu_sem.at[slot],
                ).start()

    step = 256
    blocks = [pl.ds(i * step, step) for i in range(total // step)]
    pltpu.make_async_copy(wo, wo, wo_sem).wait()
    for rows in blocks:
        unit, rate = normalise(mixed_ref[rows, :].astype(f32) + dot(ctx_ref[rows, :], wo[...]) + ob)
        unit_ref[rows, :] = unit
        rate_ref[rows, :] = rate
        normed = unit * g1 + s1
        low_ref[rows, :] = normed.astype(bf16)
        first_ref[rows, :] = normed + ub
    for slot in range(WIDTHS):
        quarter = own ^ slot
        pltpu.make_async_copy(wi.at[slot], wi.at[slot], wi_sem.at[slot]).wait()
        pltpu.make_async_copy(wu.at[slot], wu.at[slot], wu_sem.at[slot]).wait()

        @pl.when(quarter < active)
        def _():
            bias = bi_ref[quarter].astype(f32)
            for rows in blocks:
                inner = dot(low_ref[rows, :], wi[slot]) + bias
                phi = 0.5 * (1.0 + lax.erf(inner * 0.7071067811865476))
                act[slot, rows, :] = (inner * phi).astype(bf16)
                density = jnp.exp(-0.5 * inner * inner) * 0.3989422804014327
                slope[slot, rows, :] = (phi + inner * density).astype(bf16)
            first_ref[...] += dot(act[slot], wu[slot])

    sums_ref[...] = jnp.zeros_like(sums_ref)
    for rows in blocks:
        unit, rate = normalise(first_ref[rows, :])
        out_ref[rows, :] = (unit * g2 + s2).astype(bf16)
        cot = cot_ref[rows, :].astype(f32)
        grad = norm_back(cot, g2, unit, rate)
        grad_ref[rows, :] = grad
        low = grad.astype(bf16)
        glow_ref[rows, :] = low
        sums_ref[3:4, :] += col_sum(low.astype(f32))
        sums_ref[4:5, :] += col_sum(cot * unit)
        sums_ref[5:6, :] += col_sum(cot)
    first_ref[...] = grad_ref[...]

    for slot in range(WIDTHS):
        quarter = own ^ slot

        if slot > 0:
            for _ in range(2):
                pltpu.make_async_copy(stage.at[0], stage.at[0], out_sem).wait()

        @pl.when(quarter >= active)
        def _():
            stage[...] = jnp.zeros_like(stage)
            dbi_ref[quarter] = jnp.zeros((1, width), f32)

        @pl.when(quarter < active)
        def _():
            stage[1] = dot(act[slot], glow_ref[...], TN).astype(bf16)
            inner = (dot(glow_ref[...], wu[slot], NT) * slope[slot].astype(f32)).astype(bf16)
            dbi_ref[quarter] = col_sum(inner.astype(f32))
            stage[0] = dot(low_ref[...], inner, TN).astype(bf16)
            first_ref[...] += dot(inner, wi[slot], NT)

        to = (keep_i, send_i)[slot & 1]
        for piece in range(PIECES):
            pltpu.make_async_copy(
                stage.at[0, pl.ds(piece * unit_rows, unit_rows), :],
                to.at[slot >> 1, slot_of(piece, home)],
                out_sem,
            ).start()
        for end in range(2):
            for part in range(WIDTHS):
                at = pl.multiple_of(end * outer_rows + (own ^ part) * unit_rows, 16)
                pltpu.make_async_copy(
                    stage.at[1, pl.ds(at, unit_rows), :],
                    (keep_u, send_u)[part & 1].at[part >> 1, slot_of(2 * quarter + end, home)],
                    out_sem,
                ).start()

    for rows in blocks:
        unit = unit_ref[rows, :]
        normed_grad = first_ref[rows, :]
        first = norm_back(normed_grad, g1, unit, rate_ref[rows, :])
        first_ref[rows, :] = first
        low = first.astype(bf16)
        glow_ref[rows, :] = low
        dctx = dot(low, wo[...], NT)
        lane = lax.broadcasted_iota(jnp.int32, dctx.shape, 1)
        dctx_ref[rows, :] = jnp.where(lane < heads * HEAD_DIM, dctx, 0.0).astype(bf16)
        sums_ref[0:1, :] += col_sum(low.astype(f32))
        sums_ref[1:2, :] += col_sum(normed_grad * unit)
        sums_ref[2:3, :] += col_sum(normed_grad)
    dwo_ref[...] = dot(ctx_ref[...], glow_ref[...], TN).astype(bf16)
    for _ in range(2):
        pltpu.make_async_copy(stage.at[0], stage.at[0], out_sem).wait()


def feed(sc, mixed, ctx, cot, bi, vec, sources):
    total, width = mixed.shape
    square = whole((total, width))
    piece = (2, PIECES, width // PIECES, width)
    units = WIDTHS * width
    return pl.pallas_call(
        feed_kernel,
        in_specs=[SMEM, square, square, square, whole(bi.shape), whole(vec.shape)] + [ANY] * 4,
        out_specs=[square, square, square, whole((width, width)), whole((WIDTHS, 1, width)), whole((8, width))]
        + [ANY] * 4,
        out_shape=[
            shape_of((total, width)), shape_of((total, width), f32), shape_of((total, width)),
            shape_of((width, width)), shape_of((WIDTHS, 1, width), f32), shape_of((8, width), f32),
        ] + [shape_of(piece)] * 4,
        scratch_shapes=[
            pltpu.VMEM((WIDTHS, width, width), bf16), pltpu.VMEM((WIDTHS, width, width), bf16),
            pltpu.VMEM((width, width), bf16),
            pltpu.VMEM((WIDTHS, total, width), bf16), pltpu.VMEM((WIDTHS, total, width), bf16),
            pltpu.VMEM((total, width), f32), pltpu.VMEM((total, width), f32),
            pltpu.VMEM((total, width), bf16), pltpu.VMEM((total, width), bf16), pltpu.VMEM((total, 1), f32),
            pltpu.VMEM((2, width, width), bf16),
            pltpu.SemaphoreType.DMA, pltpu.SemaphoreType.DMA((WIDTHS,)), pltpu.SemaphoreType.DMA((WIDTHS,)),
            pltpu.SemaphoreType.DMA,
        ],
        compiler_params=params(60),
        cost_estimate=cost(2 * total * width * (6 * units + 3 * width), 40 * width * width, total * units),
        name="feed",
    )(sc, mixed, ctx, cot, bi, vec, *sources)


def project_grad_kernel(with_output, sc, mixed_ref, dq, dk, dv, *refs):
    dwo_ref = refs[0] if with_output else None
    keep, send, sums_ref = refs[-3:]
    width = mixed_ref.shape[1]
    part = dq.shape[1]
    rows = width // PIECES
    own, home = sc[0] & 1, sc[1]
    sums_ref[...] = jnp.zeros_like(sums_ref)

    def put(value, lanes, piece_of=lambda p: p):
        for piece in range(PIECES):
            slot = slot_of(piece, home)
            low = value[piece * rows : piece * rows + rows // 2]
            high = value[piece * rows + rows // 2 : (piece + 1) * rows]

            @pl.when(own == 0)
            def _():
                keep[slot, : rows // 2, lanes] = low
                send[slot, : rows // 2, lanes] = high

            @pl.when(own == 1)
            def _():
                keep[slot, : rows // 2, lanes] = high
                send[slot, : rows // 2, lanes] = low

    mixed = mixed_ref[...]
    for i, ref in enumerate((dq, dk, dv)):
        put(dot(mixed, ref[...], TN).astype(bf16), slice(i * part, (i + 1) * part))
        sums_ref[i : i + 1, :] = col_sum(ref[...].astype(f32))
    if with_output:
        put(dwo_ref[...], slice(3 * part, 3 * part + width))


def project_grad(sc, mixed, grads, dwo=None):
    total, width = mixed.shape
    part = grads[0].shape[1]
    rows = width // PIECES // 2
    columns = 3 * part + (0 if dwo is None else width)
    extra = [] if dwo is None else [dwo]
    pack = (PIECES, rows, columns)
    return pl.pallas_call(
        functools.partial(project_grad_kernel, dwo is not None),
        in_specs=[SMEM, whole((total, width))] + [whole((total, part))] * 3 + [whole(a.shape) for a in extra],
        out_specs=[whole(pack), whole(pack), whole((8, part))],
        out_shape=[shape_of(pack), shape_of(pack), shape_of((8, part), f32)],
        compiler_params=params(40),
        cost_estimate=cost(6 * total * width * part, 4 * total * width),
        name="project_grad",
    )(sc, mixed, *grads, *extra)


def input_grad_kernel(
    sc, src_row, first_ref, q0, k0, v0, q1, k1, v1, own, other, out_ref, weights, grads, hi_ref, lo_ref, sem
):
    total, width = first_ref.shape
    block = pl.program_id(0)
    rows = out_ref.shape[0]
    part = q0.shape[1]

    @pl.when(block == 0)
    def _():
        fetch_halves(sc, (own, other), weights, sem)
        for half, refs in enumerate(((q0, k0, v0), (q1, k1, v1))):
            for i, ref in enumerate(refs):
                grads[half, :, i * part : (i + 1) * part] = ref[...]
        pltpu.make_async_copy(weights, weights, sem).wait()
        grad = first_ref[...] + dot(grads[0], weights[0], NT) + dot(grads[1], weights[1], NT)
        hi = grad.astype(bf16)
        hi_ref[...] = hi
        lo_ref[...] = (grad - hi.astype(f32)).astype(bf16)

    target = lax.broadcasted_iota(jnp.int32, (rows, total), 0) + block * rows
    place = jnp.where(target == src_row[...], 1.0, 0.0).astype(bf16)
    out_ref[...] = dot(place, hi_ref[...]) + dot(place, lo_ref[...])


def input_grad(sc, src_row, first, halves, own, other, tile=512):
    total, width = first.shape
    part = halves[0][0].shape[1]
    columns = own.shape[2]
    return pl.pallas_call(
        input_grad_kernel,
        grid=(total // tile,),
        in_specs=[SMEM, whole(src_row.shape), whole((total, width))] + [whole((total, part))] * 6 + [ANY, ANY],
        out_specs=pl.BlockSpec((tile, width), lambda i: (i, 0)),
        out_shape=shape_of((total, width), f32),
        scratch_shapes=[
            pltpu.VMEM((2, width, columns), bf16), pltpu.VMEM((2, total, columns), bf16),
            pltpu.VMEM((total, width), bf16), pltpu.VMEM((total, width), bf16),
            pltpu.SemaphoreType.DMA,
        ],
        compiler_params=params(52),
        cost_estimate=cost(4 * total * width * columns + 4 * total * total * width, 20 * total * width),
        name="input_grad",
    )(sc, src_row, first, *halves[0], *halves[1], own, other)


def finish_kernel(
    sc, feed0, feed1, feed2, feed3, low_own, low_other, high_own, high_other,
    gq, gk, gv, go, gi, gu, *vectors,
):
    own = sc[0]
    rows, width = gq.shape
    half, part = rows // 2, width // 2
    for slot, ref in enumerate((feed0, feed1, feed2, feed3)):
        quarter = own ^ slot
        at = pl.multiple_of(quarter * width, 128)
        gi[:, pl.ds(at, width)] = ref[0].astype(f32)
        to = pl.multiple_of(quarter * rows, 8)
        gu[pl.ds(to, rows), :] = ref[1].astype(f32)
    for other, (low, high) in enumerate(((low_own, high_own), (low_other, high_other))):
        to = pl.ds(pl.multiple_of(((own & 1) ^ other) * half, 8), half)
        for i, ref in enumerate((gq, gk, gv)):
            ref[to, :part] = low[:half, i * part : (i + 1) * part].astype(f32)
            ref[to, part:] = high[:half, i * part : (i + 1) * part].astype(f32)
        go[to, :] = low[:half, 3 * part :].astype(f32)
    line = jnp.where(
        (own & 1) == 0, high_own[half : half + 16, :].astype(f32), high_other[half : half + 16, :].astype(f32)
    )
    at = 0
    for ref in vectors:
        size = ref.shape[1]
        ref[...] = line[0:1, at : at + size]
        at += size


def finish(sc, feeds, lows, highs, rows, width):
    sizes = [rows] * 8 + [WIDTHS * rows]
    shapes = [(rows, width)] * 4 + [(rows, WIDTHS * width), (WIDTHS * rows, width)] + [(1, n) for n in sizes]
    inputs = [*feeds, *lows, *highs]
    return pl.pallas_call(
        finish_kernel,
        in_specs=[SMEM] + [whole(a.shape) for a in inputs],
        out_specs=[whole(s) for s in shapes],
        out_shape=[shape_of(s, f32) for s in shapes],
        compiler_params=params(24),
        cost_estimate=cost(rows * width, 60 * rows * width),
        name="finish",
    )(sc, *inputs)


def exchange(value, axis, bits):
    size = lax.axis_size(axis)
    return lax.ppermute(value, axis, [(i, i ^ bits) for i in range(size)])


def gather_pieces(piece):
    column = jnp.stack([piece] + [exchange(piece, "dp", 2 * k) for k in (1, 2, 3)])
    return column, exchange(column, "dp", 1)


def add(*terms):
    total = terms[0].astype(f32)
    for term in terms[1:]:
        total = total + term.astype(f32)
    return total.astype(bf16)


def scatter_dp(value, axis=0):
    kept = lax.slice_in_dim(value, 0, 4, axis=axis)
    sent = lax.slice_in_dim(value, 4, 8, axis=axis)
    total = add(kept, exchange(sent, "dp", 1))
    pick = lambda k: lax.index_in_dim(total, k, axis=axis, keepdims=False)
    return add(pick(0), *[exchange(pick(k), "dp", 2 * k) for k in (1, 2, 3)])


def per_device(
    inputs, cotangent, replacement_ids, augmented_count, segment_ids,
    query_weight, key_weight, value_weight, output_weight, inner_weight, outer_weight,
    query_bias, value_bias, output_bias, inner_bias, outer_bias,
    attention_gain, attention_shift, feed_gain, feed_shift,
):
    total, width = inputs.shape[1:]
    group = lax.axis_index("width")
    groups = lax.axis_size("width")
    shards = lax.axis_size("dp")
    direct = shards == PIECES and groups == WIDTHS
    rows = query_weight.shape[0]
    part = width // 2
    heads = HEADS * (group + 1) // groups
    place = lax.axis_index("dp")
    own, home = (group, place) if direct else (jnp.zeros_like(group), jnp.zeros_like(place))
    sc = jnp.stack([own, home, group + 1, heads]).astype(jnp.int32)

    positions = jnp.arange(total, dtype=jnp.int32)
    sources = jnp.where(positions < augmented_count[0, 0], replacement_ids[0], positions)
    segments = segment_ids[0, 0]
    seg_col, seg_row = segments[:, None], segments[None, :]
    windows = window_table(segments)
    mixed = mix(sources[:, None], inputs[0])

    vectors = (query_bias, value_bias, output_bias, attention_gain, attention_shift,
               outer_bias, feed_gain, feed_shift, inner_bias)
    if direct:
        line = jnp.concatenate(vectors)[None]
        start = (group & 1) * part
        cut = [lax.dynamic_slice_in_dim(a, start, part, 1) for a in (query_weight, key_weight, value_weight)]
        pack = jnp.concatenate([jnp.concatenate(cut, 1), line, jnp.zeros((15, 3 * part), bf16)])
        near, far = gather_pieces(pack)
        qkv_own = jnp.concatenate([near, far])
        qkv_other = exchange(qkv_own, "width", 1)
        feed_pack = jnp.concatenate([
            lax.dynamic_slice_in_dim(inner_weight, group * width, width, 1),
            lax.dynamic_slice_in_dim(outer_weight, group * rows, rows, 0),
            lax.dynamic_slice_in_dim(output_weight, (group & 1) * (rows // 2), rows // 2, 0),
        ])
        near, far = gather_pieces(feed_pack)
        feed0 = jnp.concatenate([near, far])
        feed2 = exchange(feed0, "width", 2)
        feed1 = exchange(feed0, "width", 1)
        feed3 = exchange(feed2, "width", 1)
        order = jnp.stack([slot_of(p, home) for p in range(PIECES)])
        lines = jnp.take(qkv_own[:, rows, :], order, axis=0)
    else:
        everything = lambda a: lax.all_gather(a, "dp", axis=0, tiled=True)
        slots = [(s & 3) * 2 + (s >> 2) for s in range(PIECES)]
        by_piece = lambda a: jnp.stack([a.reshape(PIECES, -1, a.shape[-1])[p] for p in slots])
        full = [everything(a) for a in (query_weight, key_weight, value_weight)]
        qkv_own, qkv_other = (
            by_piece(jnp.concatenate([a[:, h * part : (h + 1) * part] for a in full], 1)) for h in range(2)
        )
        piece_rows = width // PIECES
        inner_full, outer_full, output_full = (
            everything(a) for a in (inner_weight, outer_weight, output_weight)
        )
        outer_parts = by_piece(outer_full).reshape(PIECES, WIDTHS, piece_rows, width)
        output_parts = by_piece(output_full).reshape(PIECES, 2, piece_rows // 2, width)
        feed0, feed1, feed2, feed3 = (
            jnp.concatenate([
                by_piece(inner_full[:, q * width : (q + 1) * width]),
                outer_parts[:, q],
                output_parts[:, q & 1],
            ], 1)
            for q in range(WIDTHS)
        )
        lines = jnp.concatenate([everything(a).reshape(PIECES, -1) for a in vectors], 1)
    small = lines[:, :width].reshape(PIECES, 8, width // PIECES).transpose(1, 0, 2).reshape(8, width)
    inner_bias_full = lines[:, width:].reshape(WIDTHS, 1, width)
    none = jnp.zeros((part,), bf16)
    qkv_bias = jnp.stack([
        jnp.concatenate([small[0, h * part : (h + 1) * part], none, small[1, h * part : (h + 1) * part]])
        for h in range(2)
    ])
    vec = small[2:]

    q, k, v = project(sc, mixed, qkv_bias, qkv_own, qkv_other)
    ctx, lse = attend(sc, windows, seg_col, seg_row, q, k, v)
    out, first, dctx, dwo, dbi, sums, keep_i, send_i, keep_u, send_u = feed(
        sc, mixed, ctx, cotangent[0], inner_bias_full, vec, (feed0, feed1, feed2, feed3)
    )
    low = attend_back(0, sc, windows, seg_col, seg_row, q, k, v, dctx, lse)
    keep_low, send_low, sums_low = project_grad(sc, mixed, low, dwo)
    high = attend_back(1, sc, windows, seg_col, seg_row, q, k, v, dctx, lse)
    keep_high, send_high, sums_high = project_grad(sc, mixed, high)
    input_gradient = input_grad(sc, sources[None, :], first, (low, high), qkv_own, qkv_other)

    vector_grads = [
        jnp.concatenate([sums_low[0], sums_high[0]]), jnp.concatenate([sums_low[2], sums_high[2]]),
        sums[0], sums[1], sums[2], sums[3], sums[4], sums[5],
    ]
    grad_lines = jnp.concatenate(
        [jnp.stack(vector_grads).reshape(8, PIECES, -1).transpose(1, 0, 2).reshape(PIECES, width),
         dbi.reshape(PIECES, -1)], 1)
    if direct:
        part_i = add(keep_i, exchange(send_i, "width", 1))
        part_u = add(keep_u, exchange(send_u, "width", 1))
        part_i = add(part_i[0], exchange(part_i[1], "width", 2))
        part_u = scatter_dp(part_u, axis=1)
        part_i = scatter_dp(part_i)
        part_u = add(part_u[0], exchange(part_u[1], "width", 2))
        feed_sum0 = jnp.stack([part_i, part_u])
        feed_sum2 = exchange(feed_sum0, "width", 2)
        feed_sum1 = exchange(feed_sum0, "width", 1)
        feed_sum3 = exchange(feed_sum2, "width", 1)
        low_sum = scatter_dp(add(keep_low, exchange(send_low, "width", 1)))
        low_sum = add(low_sum, exchange(low_sum, "width", 2))
        low_other = exchange(low_sum, "width", 1)
        lines_slot = jnp.take(grad_lines, jnp.stack([((s & 3) ^ (home >> 1)) * 2 + ((s >> 2) ^ (home & 1)) for s in range(PIECES)]), axis=0)
        lines_slot = jnp.pad(lines_slot.astype(bf16)[:, None], ((0, 0), (0, 15), (0, 0)))
        blank = jnp.zeros_like(lines_slot)
        even = (group & 1) == 0
        keep_high = jnp.concatenate([keep_high, jnp.where(even, lines_slot, blank)], 1)
        send_high = jnp.concatenate([send_high, jnp.where(even, blank, lines_slot)], 1)
        high_sum = scatter_dp(add(keep_high, exchange(send_high, "width", 1)))
        high_sum = add(high_sum, exchange(high_sum, "width", 2))
        high_other = exchange(high_sum, "width", 1)
        results = finish(
            sc, (feed_sum0, feed_sum1, feed_sum2, feed_sum3), (low_sum, low_other), (high_sum, high_other),
            rows, width)
        matrices, lines_out = results[:6], [a[0] for a in results[6:]]
        (gq, gk, gv, go, gi, gu) = matrices
        (bq, bv, bo, ga, sa, bu, gf, sf, bi) = lines_out
    else:
        ordered = [(p & 1) * 4 + (p >> 1) for p in range(PIECES)]
        back = lambda a: jnp.stack([a[s] for s in ordered])
        total_sum = lambda a: lax.psum(lax.psum_scatter(a.astype(f32), "dp", scatter_dimension=0, tiled=True), "width")
        quarters_i = [keep_i[0], send_i[0], keep_i[1], send_i[1]]
        quarters_u = [keep_u[0], send_u[0], keep_u[1], send_u[1]]
        gi = total_sum(jnp.concatenate([back(a).reshape(width, width) for a in quarters_i], 1))
        gu = total_sum(jnp.stack([back(a) for a in quarters_u], 1).reshape(-1, width))
        low_full = jnp.concatenate([back(keep_low), back(send_low)], 1).reshape(width, -1)
        high_full = jnp.concatenate([back(keep_high), back(send_high)], 1).reshape(width, -1)
        gq, gk, gv = (
            total_sum(jnp.concatenate([a[:, i * part : (i + 1) * part] for a in (low_full, high_full)], 1))
            for i in range(3)
        )
        go = total_sum(low_full[:, 3 * part :])
        bq, bv, bo, ga, sa, bu, gf, sf = (total_sum(a) for a in vector_grads)
        bi = total_sum(dbi.reshape(-1))
    return (out[None], input_gradient[None], gq, gk, gv, go, gi, gu, bq, bv, bo, bi, bu, ga, sa, gf, sf)


def window_table(segments):
    total = segments.shape[0]
    blocks = segments.reshape(total // QB, QB)
    low = jnp.sum((segments[None, :] < blocks[:, :1]).astype(jnp.int32), axis=1)
    high = jnp.sum((segments[None, :] <= blocks[:, -1:]).astype(jnp.int32), axis=1)
    start = low // 128 * 128
    size = (high - start + QB - 1) // QB * QB
    return jnp.stack([jnp.minimum(start, total - size), size])


def solution(mesh):
    tokens = (P("width", "dp", None),) * 2 + (P("width", "dp"),) * 2 + (P("width", "dp", None),)
    matrices = (P("dp", None),) * 6
    vectors = (P("dp"),) * 9
    return jax.shard_map(
        per_device,
        mesh=mesh,
        in_specs=tokens + matrices + vectors,
        out_specs=(P("width", "dp", None),) * 2 + matrices + vectors,
        check_vma=False,
    )
```

time: 1230 us -> 491 us (0.40)
  waiting for transfers between devices: 559 us -> 171 us
  matrix products: 304 us -> 0 us
  starting transfers between devices: 0.52 us -> 147 us
  Pallas kernels: 0 us -> 125 us
  blocking collectives: 108 us -> 0 us
  local copies, waits for them, and re-layouts: 129 us -> 30.2 us
  other arithmetic: 103 us -> 10.4 us
  between operations: 18.1 us -> 2.58 us
    reduce_scatter x6 -> x0, waiting for transfers between devices: 510 us -> none  [the longest x1 166 us: per_device(): lax.psum_scatter(inner_weight_grad, 'dp', scatter_dimension=0, tiled=True)]
    dot_general x32 -> x0, matrix products: 304 us -> none  [the longest x6 63 us: product(): return jnp.dot(matrix, second, preferred_element_type=jnp.float32)]
    ppermute x0 -> x41, waiting for transfers between devices: none -> 171 us  [exchange(): return lax.ppermute(value, axis, [(i, i ^ bits) for i in range(size)])]
    ppermute x0 -> x41, starting transfers between devices: none -> 147 us  [exchange(): return lax.ppermute(value, axis, [(i, i ^ bits) for i in range(size)])]
    pallas_call x0 -> x10, Pallas kernels: none -> 125 us  [the longest x2 36 us: attend_back(): pl.pallas_call(functools.partial(attend_back_kernel, first), grid=(pairs,...]
    unnamed x2 -> x0, blocking collectives: 74.9 us -> none
    dynamic_update_slice x4 -> x0, local copies, waits for them, and re-layouts: 60.9 us -> none  [per_device(): lax.scan(attend, jnp.zeros((), jnp.float32), (query_blocks, segment_blocks))]
    convert_element_type x15, other arithmetic: 53.6 us -> 3.65 us  [the longest x14 3.55 us: add(): return total.astype(bf16)]
  transfers between devices with their start and end apart: 13 -> 41, of which waited for: 8 -> 18; matrix products, arithmetic and copies ran while one was open for 38% -> 6% of each run, Pallas kernels for 0% -> 9%
where the time goes in v1:
time: 491 us; the launch traced here: 485 us
  waiting for transfers between devices  171 us (35%)
  starting transfers between devices  147 us (30%)
  Pallas kernels  125 us (25%)
  local copies, waits for them, and re-layouts  30.2 us (6%)
  other arithmetic  10.4 us (2%)
    ppermute x41, waiting for transfers between devices, exchange(): return lax.ppermute(value, axis, [(i, i ^ bits) for i in range(size)])  171 us
    ppermute x41, starting transfers between devices, exchange(): return lax.ppermute(value, axis, [(i, i ^ bits) for i in range(size)])  147 us
    pallas_call x2, Pallas kernels, attend_back(): pl.pallas_call(functools.partial(attend_back_kernel, first), grid=(pairs,...  36 us
    pallas_call x1, Pallas kernels, feed(): pl.pallas_call(feed_kernel, in_specs=[SMEM, square, square, square, whole...  32.3 us
    pallas_call x1, Pallas kernels, attend(): pl.pallas_call(attend_kernel, grid=(pairs,), in_specs=[SMEM, SMEM, whole(...  21 us
    unnamed x88, local copies, waits for them, and re-layouts  14.6 us
    pallas_call x1, Pallas kernels, input_grad(): pl.pallas_call(input_grad_kernel, grid=(total // tile,), in_specs=[SMEM,...  14.1 us
  transfers between devices with their start and end apart: 41, of which 18 were waited for; matrix products, arithmetic and copies ran while one was open for 6% of the time, Pallas kernels for 9%

profile of v1, /device:TPU:0, one launch (start us, length us, event | category | flops | bytes accessed | tf_op | source)
XLA Modules:
  0.0 484.9 jit_solution(14909052090772221769)
XLA Ops:
  8.7 6.1 %concatenate.85 = bf16[1152]{0:T(1024)(128)(2,1)S(1)} concatenate(bf16[96]{0:T(256)(128)(2,1)} %param.31, bf16[96]{0:T(256)(128)(2,1)} %param.32, bf16[96]{0:T(256)(128)(2,1)} %param.33, bf16[96]{0:T(256)(128)(2,1)} %param.36, bf16[96]{0:T(256)(128)(2,1)} %param.37, bf16[96]{0:T(256)(128)(2,1)} %param.35, bf16[96]{0:T(256)(128)(2,1)} %param.38, bf16[96]{0:T(256)(128)(2,1)} %param.39, ...), dimensions={0} | concatenate | bytes 4608 | tf_op jit(solution)/shard_map/concatenate | solution.py:628
  15.8 5.7 %collective-permute-done.5 = bf16[240,768]{1,0:T(8,128)(2,1)S(1)} collective-permute-done((bf16[240,768]{1,0:T(8,128)(2,1)S(1)}, bf16[240,768]{1,0:T(8,128)(2,1)S(1)}, u32[]{:S(2)}, u32[]{:S(2)}) %collective-permute-start.5) | collective-permute-done | bytes 368672 | tf_op jit(solution)/shard_map/ppermute | solution.py:577
  21.5 12.5 %collective-permute-done.6 = bf16[240,768]{1,0:T(8,128)(2,1)S(1)} collective-permute-done((bf16[240,768]{1,0:T(8,128)(2,1)S(1)}, bf16[240,768]{1,0:T(8,128)(2,1)S(1)}, u32[]{:S(2)}, u32[]{:S(2)}) %collective-permute-start.6) | collective-permute-done | bytes 368672 | tf_op jit(solution)/shard_map/ppermute | solution.py:577
  36.9 7.1 %collective-permute-start = (bf16[112,1152]{1,0:T(8,128)(2,1)S(1)}, bf16[112,1152]{1,0:T(8,128)(2,1)}, u32[]{:S(2)}, u32[]{:S(2)}) collective-permute-start(bf16[112,1152]{1,0:T(8,128)(2,1)S(1)} %get-tuple-element.112), channel_id=1, source_target_pairs={{0,2},{1,3},{2,0},{3,1},{4,6},{5,7},{6,4},{7,5},{8,10},{9,11},{10,... | collective-permute-start | bytes 774152 | tf_op jit(solution)/shard_map/ppermute | solution.py:577
  52.5 14.7 %collective-permute-done.8 = bf16[4,240,768]{2,1,0:T(8,128)(2,1)} collective-permute-done((bf16[4,240,768]{2,1,0:T(8,128)(2,1)}, bf16[4,240,768]{2,1,0:T(8,128)(2,1)}, u32[]{:S(2)}, u32[]{:S(2)}) %collective-permute-start.8) | collective-permute-done | bytes 1474592 | tf_op jit(solution)/shard_map/ppermute | solution.py:577
  78.5 16.5 %collective-permute-done.3 = bf16[4,112,1152]{2,1,0:T(8,128)(2,1)S(1)} collective-permute-done((bf16[4,112,1152]{2,1,0:T(8,128)(2,1)S(1)}, bf16[4,112,1152]{2,1,0:T(8,128)(2,1)S(1)}, u32[]{:S(2)}, u32[]{:S(2)}) %collective-permute-start.3) | collective-permute-done | bytes 1032224 | tf_op jit(solution)/shard_map/ppermute | solution.py:577
  95.8 36.5 %collective-permute-done.10.f2 = bf16[8,240,768]{2,1,0:T(8,128)(2,1)} collective-permute-done((bf16[8,240,768]{2,1,0:T(8,128)(2,1)}, bf16[8,240,768]{2,1,0:T(8,128)(2,1)}, u32[]{:S(2)}, u32[]{:S(2)}) %collective-permute-start.10) | collective-permute-done | bytes 2949152 | tf_op jit(solution)/shard_map/ppermute | solution.py:577
  141.0 8.8 %project.1 = (bf16[1024,768]{1,0:T(8,128)(2,1)S(1)}, bf16[1024,768]{1,0:T(8,128)(2,1)S(1)}, bf16[1024,768]{1,0:T(8,128)(2,1)S(1)}) custom-call(s32[4]{0:T(128)S(1)} %pad_add_fusion.1.sc, bf16[1024,768]{1,0:T(8,128)(2,1)S(1)} %copy-done.10, bf16[2,1152]{1,0:T(2,128)(2,1)S(1)} %pad_maximum_fusion.8.bias_ref, ...), custom_call_target="tpu_custom_call" | custom-call | flops 3623878656 | bytes 9437184 | tf_op jit(solution)/shard_map/project/pallas_call | solution.py:102
  149.9 21.0 %attend.1 = (bf16[1024,768]{1,0:T(8,128)(2,1)S(1)}, f32[6,2,1024]{2,1,0:T(2,128)S(1)}) custom-call(s32[4]{0:T(128)S(1)} %pad_add_fusion.1.sc, s32[2,4]{1,0:T(2,128)S(1)} %pad_add_fusion.windows, s32[1024,1]{1,0:T(8,128)S(1)} %copy.58.seg_col, s32[1,1024]{1,0:T(1,128)S(1)} %bitcast.176, bf16[1024,768]{1,0:T(8,128)(2,1)S(1)} %get-tuple-element.59.q_ref, ...), custom_call_target="tpu_custom_call" | custom-call | flops 12884901888 | bytes 6291456 | tf_op jit(solution)/shard_map/attend/pallas_call | solution.py:170
  172.1 32.3 %feed.1 = (bf16[1024,768]{1,0:T(8,128)(2,1)}, f32[1024,768]{1,0:T(8,128)}, bf16[1024,768]{1,0:T(8,128)(2,1)}, bf16[768,768]{1,0:T(8,128)(2,1)}, f32[4,1,768]{2,1...) custom-call(s32[4]{0:T(128)} %copy-done.4, ...), custom_call_target="tpu_custom_call" | custom-call | flops 32614907904 | bytes 23592960 | tf_op jit(solution)/shard_map/feed/pallas_call | solution.py:409
  205.8 22.0 %attend_back.3 = (bf16[1024,384]{1,0:T(8,128)(2,1)S(1)}, bf16[1024,384]{1,0:T(8,128)(2,1)S(1)}, bf16[1024,384]{1,0:T(8,128)(2,1)S(1)}) custom-call(s32[4]{0:T(128)S(1)} %copy-done.5, s32[2,4]{1,0:T(2,128)S(1)} %pad_add_fusion.windows, s32[1024,1]{1,0:T(8,128)S(1)} %copy.58.seg_col, s32[1,1024]{1,0:T(1,128)S(1)} %bitcast.177, ...), custom_call_target="tpu_custom_call" | custom-call | flops 16106127360 | bytes 6291456 | tf_op jit(solution)/shard_map/attend_back/pallas_call | solution.py:235
  227.9 14.0 %attend_back.2 = (bf16[1024,384]{1,0:T(8,128)(2,1)S(1)}, bf16[1024,384]{1,0:T(8,128)(2,1)S(1)}, bf16[1024,384]{1,0:T(8,128)(2,1)S(1)}) custom-call(s32[4]{0:T(128)S(1)} %copy-done.5, s32[2,4]{1,0:T(2,128)S(1)} %pad_add_fusion.windows, s32[1024,1]{1,0:T(8,128)S(1)} %copy.58.seg_col, s32[1,1024]{1,0:T(1,128)S(1)} %bitcast.178, ...), custom_call_target="tpu_custom_call" | custom-call | flops 16106127360 | bytes 6291456 | tf_op jit(solution)/shard_map/attend_back/pallas_call | solution.py:235
  252.7 18.4 %collective-permute-start.34 = (bf16[8,64,1152]{2,1,0:T(8,128)(2,1)S(1)}, bf16[8,64,1152]{2,1,0:T(8,128)(2,1)S(1)}, u32[]{:S(2)}, u32[]{:S(2)}) collective-permute-start(bf16[8,64,1152]{2,1,0:T(8,128)(2,1)S(1)} %pad_maximum_fusion.1), channel_id=1, source_target_pairs={{0,8},{8,0},{16,24},{24,16},{1,9},{9,1},{17,25},{25,17},{2,10},{10... | collective-permute-start | bytes 3538952 | tf_op jit(solution)/shard_map/ppermute | solution.py:577
  276.0 13.6 %collective-permute-done.35 = bf16[4,64,1152]{2,1,0:T(8,128)(2,1)S(1)} collective-permute-done((bf16[4,64,1152]{2,1,0:T(8,128)(2,1)S(1)}, bf16[4,64,1152]{2,1,0:T(8,128)(2,1)S(1)}, u32[]{:S(2)}, u32[]{:S(2)}) %collective-permute-start.35) | collective-permute-done | bytes 589856 | tf_op jit(solution)/shard_map/ppermute | solution.py:577
  289.8 9.7 %collective-permute-start.36 = (bf16[64,1152]{1,0:T(8,128)(2,1)S(1)}, bf16[64,1152]{1,0:T(8,128)(2,1)S(1)}, u32[]{:S(2)}, u32[]{:S(2)}) collective-permute-start(bf16[64,1152]{1,0:T(8,128)(2,1)S(1)} %get-tuple-element.119), channel_id=1, source_target_pairs={{0,2},{1,3},{2,0},{3,1},{4,6},{5,7},{6,4},{7,5},{8,10},{9,11},{10,... | collective-permute-start | bytes 442376 | tf_op jit(solution)/shard_map/ppermute | solution.py:577
  307.3 6.4 %collective-permute-done.37 = bf16[64,1152]{1,0:T(8,128)(2,1)S(1)} collective-permute-done((bf16[64,1152]{1,0:T(8,128)(2,1)S(1)}, bf16[64,1152]{1,0:T(8,128)(2,1)S(1)}, u32[]{:S(2)}, u32[]{:S(2)}) %collective-permute-start.37) | collective-permute-done | bytes 147488 | tf_op jit(solution)/shard_map/ppermute | solution.py:577
  313.8 57.7 %collective-permute-start.39 = (bf16[64,1152]{1,0:T(8,128)(2,1)S(1)}, bf16[64,1152]{1,0:T(8,128)(2,1)S(1)}, u32[]{:S(2)}, u32[]{:S(2)}) collective-permute-start(bf16[64,1152]{1,0:T(8,128)(2,1)S(1)} %fusion.9), channel_id=1, source_target_pairs={{0,16},{8,24},{16,0},{24,8},{1,17},{9,25},{17,1},{25,9},{2,18},{10... | collective-permute-start | bytes 442376 | tf_op jit(solution)/shard_map/ppermute | solution.py:577
  380.1 11.3 %collective-permute-done.28 = bf16[4,48,1920]{2,1,0:T(8,128)(2,1)S(1)} collective-permute-done((bf16[4,48,1920]{2,1,0:T(8,128)(2,1)S(1)}, bf16[4,48,1920]{2,1,0:T(8,128)(2,1)S(1)}, u32[]{:S(2)}, u32[]{:S(2)}) %collective-permute-start.28) | collective-permute-done | bytes 737312 | tf_op jit(solution)/shard_map/ppermute | solution.py:577
  396.6 7.6 %collective-permute-done.13 = bf16[8,96,768]{2,1,0:T(8,128)(2,1)S(1)} collective-permute-done((bf16[8,96,768]{2,1,0:T(8,128)(2,1)S(1)}, bf16[8,96,768]{2,1,0:T(8,128)(2,1)S(1)}, u32[]{:S(2)}, u32[]{:S(2)}) %collective-permute-start.13) | collective-permute-done | bytes 1179680 | tf_op jit(solution)/shard_map/ppermute | solution.py:577
  407.9 6.8 %collective-permute-done.19 = bf16[2,4,96,768]{3,2,0,1:T(8,128)(2,1)S(1)} collective-permute-done((bf16[2,4,96,768]{3,2,0,1:T(8,128)(2,1)S(1)}, bf16[2,4,96,768]{3,2,0,1:T(8,128)(2,1)S(1)}, u32[]{:S(2)}, u32[]{:S(2)}) %collective-permute-start.19) | collective-permute-done | bytes 1179680 | tf_op jit(solution)/shard_map/ppermute | solution.py:577
  423.2 7.6 %collective-permute-done.20 = bf16[2,96,768]{2,1,0:T(8,128)(2,1)S(1)} collective-permute-done((bf16[2,96,768]{2,1,0:T(8,128)(2,1)S(1)}, bf16[2,96,768]{2,1,0:T(8,128)(2,1)S(1)}, u32[]{:S(2)}, u32[]{:S(2)}) %collective-permute-start.20) | collective-permute-done | bytes 294944 | tf_op jit(solution)/shard_map/ppermute | solution.py:577
  431.5 12.6 %collective-permute-done.21 = bf16[2,96,768]{2,1,0:T(8,128)(2,1)S(1)} collective-permute-done((bf16[2,96,768]{2,1,0:T(8,128)(2,1)S(1)}, bf16[2,96,768]{2,1,0:T(8,128)(2,1)S(1)}, u32[]{:S(2)}, u32[]{:S(2)}) %collective-permute-start.21) | collective-permute-done | bytes 294944 | tf_op jit(solution)/shard_map/ppermute | solution.py:577
  452.8 7.8 %collective-permute-done.16 = bf16[96,768]{1,0:T(8,128)(2,1)S(1)} collective-permute-done((bf16[96,768]{1,0:T(8,128)(2,1)S(1)}, bf16[96,768]{1,0:T(8,128)(2,1)S(1)}, u32[]{:S(2)}, u32[]{:S(2)}) %collective-permute-start.16) | collective-permute-done | bytes 147488 | tf_op jit(solution)/shard_map/ppermute | solution.py:577
  467.5 14.1 %input_grad.1 = f32[1024,768]{1,0:T(8,128)} custom-call(s32[4]{0:T(128)S(1)} %copy-done.5, s32[1,1024]{1,0:T(1,128)S(1)} %compare_select_fusion.src_row, f32[1024,768]{1,0:T(8,128)} %get-tuple-element.64.first_ref, bf16[1024,384]{1,0:T(8,128)(2,1)S(1)} %copy-done.14, bf16[1024,384]{1,0:T(8,128)(2,1)S(1)} %copy-done.16, bf16[1024,384]{1,0:T(8,128)(2,1)} %copy-done.17, ...), custom_call_target="tpu_custom_call" | custom-call | flops 6845104128 | bytes 15728640 | tf_op jit(solution)/shard_map/input_grad/pallas_call | solution.py:514
  (255 shorter events, 111.5 us)
Async XLA Ops:
  5.8 28.2 %collective-permute-start.6 = (bf16[240,768]{1,0:T(8,128)(2,1)S(1)}, bf16[240,768]{1,0:T(8,128)(2,1)S(1)}, u32[]{:S(2)}, u32[]{:S(2)}) collective-permute-start(bf16[240,768]{1,0:T(8,128)(2,1)S(1)} %get-tuple-element.126), channel_id=1, source_target_pairs={{0,4},{1,5},{2,6},{3,7},{4,0},{5,1},{6,2},{7,3},{8,12},{9,13},{10,... | collective-permute-start | bytes 1105928 | tf_op jit(solution)/shard_map/ppermute | solution.py:577
  8.4 25.6 %collective-permute-start.7 = (bf16[240,768]{1,0:T(8,128)(2,1)S(1)}, bf16[240,768]{1,0:T(8,128)(2,1)S(1)}, u32[]{:S(2)}, u32[]{:S(2)}) collective-permute-start(bf16[240,768]{1,0:T(8,128)(2,1)S(1)} %get-tuple-element.126), channel_id=1, source_target_pairs={{0,6},{1,7},{2,4},{3,5},{4,2},{5,3},{6,0},{7,1},{8,14},{9,15},{10,... | collective-permute-start | bytes 1105928 | tf_op jit(solution)/shard_map/ppermute | solution.py:577
  35.3 31.9 %collective-permute-start.8 = (bf16[4,240,768]{2,1,0:T(8,128)(2,1)}, bf16[4,240,768]{2,1,0:T(8,128)(2,1)}, u32[]{:S(2)}, u32[]{:S(2)}) collective-permute-start(bf16[4,240,768]{2,1,0:T(8,128)(2,1)} %pad_maximum_fusion), channel_id=1, source_target_pairs={{0,1},{1,0},{2,3},{3,2},{4,5},{5,4},{6,7},{7,6},{8,9},{9,8},{10,11... | collective-permute-start | bytes 4423688 | tf_op jit(solution)/shard_map/ppermute | solution.py:577
  36.9 35.7 %collective-permute-start = (bf16[112,1152]{1,0:T(8,128)(2,1)S(1)}, bf16[112,1152]{1,0:T(8,128)(2,1)}, u32[]{:S(2)}, u32[]{:S(2)}) collective-permute-start(bf16[112,1152]{1,0:T(8,128)(2,1)S(1)} %get-tuple-element.112), channel_id=1, source_target_pairs={{0,2},{1,3},{2,0},{3,1},{4,6},{5,7},{6,4},{7,5},{8,10},{9,11},{10,... | collective-permute-start | bytes 774152 | tf_op jit(solution)/shard_map/ppermute | solution.py:577
  44.0 28.6 %collective-permute-start.1 = (bf16[112,1152]{1,0:T(8,128)(2,1)S(1)}, bf16[112,1152]{1,0:T(8,128)(2,1)}, u32[]{:S(2)}, u32[]{:S(2)}) collective-permute-start(bf16[112,1152]{1,0:T(8,128)(2,1)S(1)} %get-tuple-element.112), channel_id=1, source_target_pairs={{0,4},{1,5},{2,6},{3,7},{4,0},{5,1},{6,2},{7,3},{8,12},{9,13},{10,... | collective-permute-start | bytes 774152 | tf_op jit(solution)/shard_map/ppermute | solution.py:577
  45.5 27.1 %collective-permute-start.2 = (bf16[112,1152]{1,0:T(8,128)(2,1)S(1)}, bf16[112,1152]{1,0:T(8,128)(2,1)}, u32[]{:S(2)}, u32[]{:S(2)}) collective-permute-start(bf16[112,1152]{1,0:T(8,128)(2,1)S(1)} %get-tuple-element.112), channel_id=1, source_target_pairs={{0,6},{1,7},{2,4},{3,5},{4,2},{5,3},{6,0},{7,1},{8,14},{9,15},{10,... | collective-permute-start | bytes 774152 | tf_op jit(solution)/shard_map/ppermute | solution.py:577
  69.8 62.6 %collective-permute-start.10 = (bf16[8,240,768]{2,1,0:T(8,128)(2,1)}, bf16[8,240,768]{2,1,0:T(8,128)(2,1)}, u32[]{:S(2)}, u32[]{:S(2)}) collective-permute-start(bf16[8,240,768]{2,1,0:T(8,128)(2,1)} %constant_dynamic-update-slice_fusion.5.f0), channel_id=1, source_target_pairs={{0,16},{8,24},{16,0},{24,8},{1,17},{9,25},{17,1},{25,9},{2,18},{10... | collective-permute-start | bytes 8847368 | tf_op jit(solution)/shard_map/ppermute | solution.py:577
  74.0 20.9 %collective-permute-start.3 = (bf16[4,112,1152]{2,1,0:T(8,128)(2,1)S(1)}, bf16[4,112,1152]{2,1,0:T(8,128)(2,1)S(1)}, u32[]{:S(2)}, u32[]{:S(2)}) collective-permute-start(bf16[4,112,1152]{2,1,0:T(8,128)(2,1)S(1)} %pad_maximum_fusion.2), channel_id=1, source_target_pairs={{0,1},{1,0},{2,3},{3,2},{4,5},{5,4},{6,7},{7,6},{8,9},{9,8},{10,11... | collective-permute-start | bytes 3096584 | tf_op jit(solution)/shard_map/ppermute | solution.py:577
  95.1 44.5 %collective-permute-start.4 = (bf16[8,112,1152]{2,1,0:T(8,128)(2,1)S(1)}, bf16[8,112,1152]{2,1,0:T(8,128)(2,1)}, u32[]{:S(2)}, u32[]{:S(2)}) collective-permute-start(bf16[8,112,1152]{2,1,0:T(8,128)(2,1)S(1)} %constant_dynamic-update-slice_fusion.own), channel_id=1, source_target_pairs={{0,8},{8,0},{16,24},{24,16},{1,9},{9,1},{17,25},{25,17},{2,10},{10... | collective-permute-start | bytes 6193160 | tf_op jit(solution)/shard_map/ppermute | solution.py:577
  95.2 76.8 %collective-permute-start.9 = (bf16[8,240,768]{2,1,0:T(8,128)(2,1)}, bf16[8,240,768]{2,1,0:T(8,128)(2,1)}, u32[]{:S(2)}, u32[]{:S(2)}) collective-permute-start(bf16[8,240,768]{2,1,0:T(8,128)(2,1)} %constant_dynamic-update-slice_fusion.5.f0), channel_id=1, source_target_pairs={{0,8},{8,0},{16,24},{24,16},{1,9},{9,1},{17,25},{25,17},{2,10},{10... | collective-permute-start | bytes 8847368 | tf_op jit(solution)/shard_map/ppermute | solution.py:577
  132.3 39.7 %collective-permute-start.11 = (bf16[8,240,768]{2,1,0:T(8,128)(2,1)}, bf16[8,240,768]{2,1,0:T(8,128)(2,1)}, u32[]{:S(2)}, u32[]{:S(2)}) collective-permute-start(bf16[8,240,768]{2,1,0:T(8,128)(2,1)} %collective-permute-done.10.f2), channel_id=1, source_target_pairs={{0,8},{8,0},{16,24},{24,16},{1,9},{9,1},{17,25},{25,17},{2,10},{10... | collective-permute-start | bytes 8847368 | tf_op jit(solution)/shard_map/ppermute | solution.py:577
  275.5 96.0 %collective-permute-start.27 = (bf16[8,48,1920]{2,1,0:T(8,128)(2,1)S(1)}, bf16[8,48,1920]{2,1,0:T(8,128)(2,1)S(1)}, u32[]{:S(2)}, u32[]{:S(2)}) collective-permute-start(bf16[8,48,1920]{2,1,0:T(8,128)(2,1)S(1)} %copy-done.8), channel_id=1, source_target_pairs={{0,8},{8,0},{16,24},{24,16},{1,9},{9,1},{17,25},{25,17},{2,10},{10... | collective-permute-start | bytes 4423688 | tf_op jit(solution)/shard_map/ppermute | solution.py:577
  275.6 99.2 %collective-permute-start.12 = (bf16[2,8,96,768]{3,2,1,0:T(8,128)(2,1)S(1)}, bf16[2,8,96,768]{3,2,1,0:T(8,128)(2,1)S(1)}, u32[]{:S(2)}, u32[]{:S(2)}) collective-permute-start(bf16[2,8,96,768]{3,2,1,0:T(8,128)(2,1)S(1)} %copy-done.38), channel_id=1, source_target_pairs={{0,8},{8,0},{16,24},{24,16},{1,9},{9,1},{17,25},{25,17},{2,10},{10... | collective-permute-start | bytes 7077896 | tf_op jit(solution)/shard_map/ppermute | solution.py:577
  299.7 77.9 %collective-permute-start.18 = (bf16[2,8,96,768]{3,2,0,1:T(8,128)(2,1)S(1)}, bf16[2,8,96,768]{3,2,0,1:T(8,128)(2,1)S(1)}, u32[]{:S(2)}, u32[]{:S(2)}) collective-permute-start(bf16[2,8,96,768]{3,2,0,1:T(8,128)(2,1)S(1)} %copy.63), channel_id=1, source_target_pairs={{0,8},{8,0},{16,24},{24,16},{1,9},{9,1},{17,25},{25,17},{2,10},{10... | collective-permute-start | bytes 7077896 | tf_op jit(solution)/shard_map/ppermute | solution.py:577
  313.8 60.9 %collective-permute-start.39 = (bf16[64,1152]{1,0:T(8,128)(2,1)S(1)}, bf16[64,1152]{1,0:T(8,128)(2,1)S(1)}, u32[]{:S(2)}, u32[]{:S(2)}) collective-permute-start(bf16[64,1152]{1,0:T(8,128)(2,1)S(1)} %fusion.9), channel_id=1, source_target_pairs={{0,16},{8,24},{16,0},{24,8},{1,17},{9,25},{17,1},{25,9},{2,18},{10... | collective-permute-start | bytes 442376 | tf_op jit(solution)/shard_map/ppermute | solution.py:577
  374.7 106.9 %collective-permute-start.40 = (bf16[64,1152]{1,0:T(8,128)(2,1)S(1)}, bf16[64,1152]{1,0:T(8,128)(2,1)S(1)}, u32[]{:S(2)}, u32[]{:S(2)}) collective-permute-start(bf16[64,1152]{1,0:T(8,128)(2,1)S(1)} %add_convert_fusion.9.high_own), channel_id=1, source_target_pairs={{0,8},{8,0},{16,24},{24,16},{1,9},{9,1},{17,25},{25,17},{2,10},{10... | collective-permute-start | bytes 442376 | tf_op jit(solution)/shard_map/ppermute | solution.py:577
  375.6 28.6 %collective-permute-start.13 = (bf16[8,96,768]{2,1,0:T(8,128)(2,1)S(1)}, bf16[8,96,768]{2,1,0:T(8,128)(2,1)S(1)}, u32[]{:S(2)}, u32[]{:S(2)}) collective-permute-start(bf16[8,96,768]{2,1,0:T(8,128)(2,1)S(1)} %slice_bitcast_fusion), channel_id=1, source_target_pairs={{0,16},{8,24},{16,0},{24,8},{1,17},{9,25},{17,1},{25,9},{2,18},{10... | collective-permute-start | bytes 3538952 | tf_op jit(solution)/shard_map/ppermute | solution.py:577
  378.4 36.3 %collective-permute-start.19 = (bf16[2,4,96,768]{3,2,0,1:T(8,128)(2,1)S(1)}, bf16[2,4,96,768]{3,2,0,1:T(8,128)(2,1)S(1)}, u32[]{:S(2)}, u32[]{:S(2)}) collective-permute-start(bf16[2,4,96,768]{3,2,0,1:T(8,128)(2,1)S(1)} %slice.205), channel_id=1, source_target_pairs={{0,1},{1,0},{2,3},{3,2},{4,5},{5,4},{6,7},{7,6},{8,9},{9,8},{10,11... | collective-permute-start | bytes 3538952 | tf_op jit(solution)/shard_map/ppermute | solution.py:577
  391.6 25.2 %collective-permute-start.29 = (bf16[48,1920]{1,0:T(8,128)(2,1)S(1)}, bf16[48,1920]{1,0:T(8,128)(2,1)S(1)}, u32[]{:S(2)}, u32[]{:S(2)}) collective-permute-start(bf16[48,1920]{1,0:T(8,128)(2,1)S(1)} %get-tuple-element.116), channel_id=1, source_target_pairs={{0,2},{1,3},{2,0},{3,1},{4,6},{5,7},{6,4},{7,5},{8,10},{9,11},{10,... | collective-permute-start | bytes 552968 | tf_op jit(solution)/shard_map/ppermute | solution.py:577
  394.9 25.7 %collective-permute-start.30 = (bf16[48,1920]{1,0:T(8,128)(2,1)S(1)}, bf16[48,1920]{1,0:T(8,128)(2,1)S(1)}, u32[]{:S(2)}, u32[]{:S(2)}) collective-permute-start(bf16[48,1920]{1,0:T(8,128)(2,1)S(1)} %get-tuple-element.118), channel_id=1, source_target_pairs={{0,4},{1,5},{2,6},{3,7},{4,0},{5,1},{6,2},{7,3},{8,12},{9,13},{10,... | collective-permute-start | bytes 552968 | tf_op jit(solution)/shard_map/ppermute | solution.py:577
  414.7 30.0 %collective-permute-start.14 = (bf16[4,96,768]{2,1,0:T(8,128)(2,1)S(1)}, bf16[4,96,768]{2,1,0:T(8,128)(2,1)S(1)}, u32[]{:S(2)}, u32[]{:S(2)}) collective-permute-start(bf16[4,96,768]{2,1,0:T(8,128)(2,1)S(1)} %slice.199), channel_id=1, source_target_pairs={{0,1},{1,0},{2,3},{3,2},{4,5},{5,4},{6,7},{7,6},{8,9},{9,8},{10,11... | collective-permute-start | bytes 1769480 | tf_op jit(solution)/shard_map/ppermute | solution.py:577
  420.6 23.5 %collective-permute-start.21 = (bf16[2,96,768]{2,1,0:T(8,128)(2,1)S(1)}, bf16[2,96,768]{2,1,0:T(8,128)(2,1)S(1)}, u32[]{:S(2)}, u32[]{:S(2)}) collective-permute-start(bf16[2,96,768]{2,1,0:T(8,128)(2,1)S(1)} %get-tuple-element.115), channel_id=1, source_target_pairs={{0,4},{1,5},{2,6},{3,7},{4,0},{5,1},{6,2},{7,3},{8,12},{9,13},{10,... | collective-permute-start | bytes 884744 | tf_op jit(solution)/shard_map/ppermute | solution.py:577
  421.2 22.9 %collective-permute-start.22 = (bf16[2,96,768]{2,1,0:T(8,128)(2,1)S(1)}, bf16[2,96,768]{2,1,0:T(8,128)(2,1)S(1)}, u32[]{:S(2)}, u32[]{:S(2)}) collective-permute-start(bf16[2,96,768]{2,1,0:T(8,128)(2,1)S(1)} %get-tuple-element.114), channel_id=1, source_target_pairs={{0,6},{1,7},{2,4},{3,5},{4,2},{5,3},{6,0},{7,1},{8,14},{9,15},{10,... | collective-permute-start | bytes 884744 | tf_op jit(solution)/shard_map/ppermute | solution.py:577
  430.7 31.1 %collective-permute-start.32 = (bf16[48,1920]{1,0:T(8,128)(2,1)S(1)}, bf16[48,1920]{1,0:T(8,128)(2,1)S(1)}, u32[]{:S(2)}, u32[]{:S(2)}) collective-permute-start(bf16[48,1920]{1,0:T(8,128)(2,1)S(1)} %fusion.6), channel_id=1, source_target_pairs={{0,16},{8,24},{16,0},{24,8},{1,17},{9,25},{17,1},{25,9},{2,18},{10... | collective-permute-start | bytes 552968 | tf_op jit(solution)/shard_map/ppermute | solution.py:577
  (56 other events, 714.4 us)
